TPU v7x, 32 devices: a whole 2x2x4 slice. The times are simulated.
32 devices in a mesh: section: 4 (over z), dp: 2 (over x), fsdp: 4 (over y, core).
Axes of the slice: x: 2, y: 2, z: 4, core: 2. Of those that a mesh axis runs over, the one named last changes fastest.
Arguments:
- x_down: bfloat16 [4, 2, 512, 6144], P('section', 'dp', 'fsdp'), may hold values from -6 to 6
- x_up: bfloat16 [4, 2, 512, 6144], P('section', 'dp', 'fsdp'), may hold values from -6 to 6
- w_tiles: bfloat16 [4, 2, 20, 2, 128, 128], P('section', None, 'fsdp'), as said below
- tile_rows: int32 [4, 2, 20], P('section'), may hold values from 0 to 47, as said below
- tile_cols: int32 [4, 2, 20], P('section'), may hold values from 0 to 191, as said below
- counts: int32 [4, 2, 4], P('section'), may hold values from 2 to 5, as said below
Outputs:
- tile_grads: bfloat16 [4, 20, 2, 128, 128], P('section', 'fsdp')
Inputs may be any that keep to these rules, and one draw needn't show every extreme that they name: w_tiles[l, 1] equals w_tiles[(l + 2) mod 4, 0]. tile_rows[l, 1] equals tile_rows[(l + 2) mod 4, 0]; the 20 row blocks of one layer are distinct. tile_cols[l, 1] equals tile_cols[(l + 2) mod 4, 0]; every column block that a layer uses is used by exactly two of its slots. counts[l, 1] equals counts[(l + 2) mod 4, 0]; the counts of one layer are the numbers 5 - i * 5 // 4 for i < 4 in some order.
All inputs are finite; a program needn't handle non-finite values.
Results may differ from a plain program's by a relative error of at most 0.0065.
Values may be sent and summed in bfloat16 or wider, within the bound.
No kernel may reach another device: no remote copies, remote signals or barrier semaphores. Data moves between devices by JAX's collectives and lax.ppermute only.
A program may use at most 64 MiB of HBM per device.

v0:
```python
import functools
import math

import jax
import jax.numpy as jnp
from jax import lax
from jax.experimental import pallas as pl
from jax.experimental.pallas import tpu as pltpu
from jax.sharding import PartitionSpec as P

TILE = 128
PLANE = ("dp", "fsdp")
SOURCES_AT_ONCE = 4
COLUMNS = 192
CORES = 2
IN_VMEM = pltpu.CompilerParams(vmem_limit_bytes=16 * 1024 * 1024)

tanh_scale = math.sqrt(2.0 / math.pi)
cubic_coef = 0.044715


def gelu_pair(hidden):
    square = hidden * hidden
    tangent = jnp.tanh(tanh_scale * (hidden + cubic_coef * hidden * square))
    half = 0.5 * (1.0 + tangent)
    value = hidden * half
    slope = half + 0.5 * hidden * (1.0 - tangent * tangent) * tanh_scale * (
        1.0 + 3.0 * cubic_coef * square
    )
    return (value, slope)


def live_total(slots, owners):
    cap = slots // owners
    return sum(cap - i * cap // owners for i in range(owners))


def unit_place(unit, per_half, owners):
    half, at = unit // per_half, unit % per_half
    return at // CORES * owners + half * CORES + at % CORES


def unit_here(per_half, owners):
    owner = lax.axis_index("fsdp")
    at = lax.axis_index("dp") * CORES + owner % CORES
    return owner // CORES * per_half + jnp.minimum(at, per_half - 1)


def order_units(
    cols_ref, counts_ref, which, slots, per_half, order_ref, flags_ref, first_ref, last_ref
):
    per_owner, middle, unused = slots // counts_ref.shape[2], slots // 2, 4 * per_half
    for i in range(order_ref.shape[0]):
        order_ref[i] = -1
        flags_ref[i] = 0
    cols = []
    for s in range(slots):
        living = counts_ref[0, which, s // per_owner] > s % per_owner
        cols.append(jnp.where(living, cols_ref[0, which, s], COLUMNS))
    for s in range(slots):
        last_ref[cols[s]] = s
        first_ref[cols[slots - 1 - s]] = slots - 1 - s
    filled = [jnp.int32(0), jnp.int32(0)]

    def put(unit, slot_a, slot_b, coupled, really):
        at = jnp.where(really, 2 * unit, unused)
        order_ref[at] = slot_a
        order_ref[at + 1] = slot_b
        flags_ref[at] = coupled

    count = lambda condition: jnp.where(condition, 1, 0)
    alone, mixed = [], []
    for s in range(slots):
        living = cols[s] < COLUMNS
        first, last = first_ref[cols[s]], last_ref[cols[s]]
        leads = living & (first == s) & (last > s)
        alone.append(living & (first == last))
        half = s // middle
        pure = leads & (last < (half + 1) * middle)
        put(half * per_half + filled[half], s, last, 1, pure)
        filled[half] = filled[half] + count(pure)
        if half == 0:
            mixed.append((s, last, 1, leads & (last >= middle)))
    waiting, odd = [jnp.int32(0), jnp.int32(0)], [jnp.int32(0), jnp.int32(0)]
    for s in range(slots):
        half = s // middle
        second = alone[s] & (odd[half] == 1)
        put(half * per_half + filled[half], waiting[half], s, 0, second)
        filled[half] = filled[half] + count(second)
        odd[half] = jnp.where(alone[s], 1 - odd[half], odd[half])
        waiting[half] = jnp.where(alone[s], s, waiting[half])
    mixed.append((waiting[0], waiting[1], 0, odd[0] == 1))
    for low, high, coupled, really in mixed:
        room = filled[0] < per_half
        unit = jnp.where(room, filled[0], per_half + filled[1])
        put(unit, jnp.where(room, low, high), jnp.where(room, high, low), coupled, really)
        filled[0] = filled[0] + count(really & room)
        filled[1] = filled[1] + count(really & jnp.logical_not(room))


def pack_kernel(
    per_half, halfway, rows_ref, cols_ref, counts_ref, down_ref, up_ref, w_ref,
    out_ref, own_w_ref, far_w_ref, order_ref, flags_ref,
    up_order_ref, up_flags_ref, first_ref, last_ref, sems, w_sems,
):
    slots, owners = cols_ref.shape[2], counts_ref.shape[2]
    per_owner, places, units = slots // owners, out_ref.shape[0] // 2, 2 * per_half
    behind = jnp.where(lax.axis_index("section") < halfway, 0, places)
    copies = [pltpu.make_async_copy(w_ref.at[0, 0], own_w_ref, w_sems.at[CORES])]
    copies[0].start()
    used = [unit_place(unit, per_half, owners) for unit in range(units)]
    for which, x_ref, order, flags, base in (
        (1, up_ref, up_order_ref, up_flags_ref, places - behind),
        (0, down_ref, order_ref, flags_ref, behind),
    ):
        order_units(
            cols_ref, counts_ref, which, slots, per_half, order, flags, first_ref, last_ref
        )
        for i in range(2 * units):
            row = rows_ref[0, which, jnp.maximum(order[i], 0)]
            at = pl.multiple_of(row * TILE, TILE)
            copy = pltpu.make_async_copy(
                x_ref.at[0, 0, :, pl.ds(at, TILE)],
                out_ref.at[base + used[i // 2], i % 2],
                sems.at[2 * units * which + i],
            )
            copy.start()
            copies.append(copy)
    owner = lax.axis_index("fsdp")
    for core in range(CORES):
        at = jnp.minimum(lax.axis_index("dp") * CORES + core, per_half - 1)
        asker = (1 - owner // CORES) * per_half + at
        held = order_ref[2 * asker + 1] - owner * per_owner
        held = jnp.where((held >= 0) & (held < per_owner), held, 0)
        copy = pltpu.make_async_copy(w_ref.at[0, 0, held], far_w_ref.at[core], w_sems.at[core])
        copy.start()
        copies.append(copy)
    for place in range(places):
        if place not in used:
            out_ref[place] = jnp.zeros(out_ref.shape[1:], out_ref.dtype)
            out_ref[places + place] = jnp.zeros(out_ref.shape[1:], out_ref.dtype)
    for copy in copies:
        copy.wait()


def pack(x_down, x_up, w_tiles, tile_rows, tile_cols, counts, per_half, places, halfway):
    rows, units = x_down.shape[2], 2 * per_half
    smem = pl.BlockSpec(memory_space=pltpu.SMEM)
    vmem = pl.BlockSpec(memory_space=pltpu.VMEM)
    hbm = pl.BlockSpec(memory_space=pl.ANY)
    return pl.pallas_call(
        functools.partial(pack_kernel, per_half, halfway),
        out_shape=[
            jax.ShapeDtypeStruct((2 * places, 2, rows, TILE), x_down.dtype),
            jax.ShapeDtypeStruct(w_tiles.shape[2:], w_tiles.dtype),
            jax.ShapeDtypeStruct((CORES,) + w_tiles.shape[3:], w_tiles.dtype),
            jax.ShapeDtypeStruct((2 * units + 2,), jnp.int32),
            jax.ShapeDtypeStruct((2 * units + 2,), jnp.int32),
        ],
        in_specs=[smem, smem, smem, hbm, hbm, hbm],
        out_specs=[vmem, vmem, vmem, smem, smem],
        scratch_shapes=[
            pltpu.SMEM((2 * units + 2,), jnp.int32),
            pltpu.SMEM((2 * units + 2,), jnp.int32),
            pltpu.SMEM((COLUMNS + 1,), jnp.int32),
            pltpu.SMEM((COLUMNS + 1,), jnp.int32),
            pltpu.SemaphoreType.DMA((4 * units,)),
            pltpu.SemaphoreType.DMA((CORES + 1,)),
        ],
        cost_estimate=pl.CostEstimate(
            flops=0, bytes_accessed=16 * units * rows * TILE, transcendentals=0
        ),
    )(tile_rows, tile_cols, counts, x_down, x_up, w_tiles)


def swapped(array, apart):
    size = lax.axis_size("fsdp")
    return lax.ppermute(array, "fsdp", [(i, i ^ apart) for i in range(size)])


def share_weights(own_w, far_w):
    both = jnp.concatenate([own_w, swapped(far_w, CORES)], axis=0)
    return jnp.concatenate([both, swapped(both, 1)], axis=0)


def weights_at(slot, per_owner):
    me, owner = lax.axis_index("fsdp"), slot // per_owner
    here = jnp.where(owner // CORES == me // CORES, slot - owner * per_owner, per_owner + me % CORES)
    return here + jnp.where(owner % CORES == me % CORES, 0, per_owner + CORES)


def dot(a, b, over_a, over_b):
    return lax.dot_general(
        a, b, (((over_a,), (over_b,)), ((), ())), preferred_element_type=jnp.float32
    )


def grads_kernel(
    per_half, owners, loss_scale, order_ref, flags_ref, x_ref, w_ref, out_ref,
    first_sum, second_sum,
):
    sources, _, rows, _ = x_ref.shape
    per_owner = w_ref.shape[0] // 2 - CORES
    unit = unit_here(per_half, owners)
    ats = [weights_at(jnp.maximum(order_ref[2 * unit + i], 0), per_owner) for i in range(2)]
    w_own = lambda i, k: w_ref[ats[i], k]
    first_sum[...] = jnp.zeros_like(first_sum)
    second_sum[...] = jnp.zeros_like(second_sum)
    together = min(SOURCES_AT_ONCE, sources)
    steps = sources // together
    coupled = flags_ref[2 * unit] == 1

    def read(step):
        at = step * together
        return [
            x_ref[pl.ds(at, together), i].reshape(together * rows, TILE) for i in range(2)
        ]

    @pl.when(coupled)
    def _():
        def go(step, carry):
            xs = jnp.concatenate(read(step), axis=1)
            firsts = jnp.concatenate([w_own(0, 0), w_own(1, 0)], axis=0)
            seconds = jnp.concatenate([w_own(0, 1), w_own(1, 1)], axis=1)
            value, slope = gelu_pair(dot(xs, firsts, 1, 0))
            active = value.astype(jnp.bfloat16)
            delta = dot(active, seconds, 1, 0)
            cotangent = (loss_scale * (xs.astype(jnp.float32) + delta)).astype(jnp.bfloat16)
            grad_act = dot(cotangent, seconds, 1, 1)
            grad_pre = (grad_act * slope).astype(jnp.bfloat16)
            first_sum[...] += dot(xs, grad_pre, 0, 0)
            second_sum[...] += dot(active, cotangent, 0, 0)
            return carry

        lax.fori_loop(0, steps, go, 0, unroll=min(steps, 4))

    @pl.when(jnp.logical_not(coupled))
    def _():
        def go(step, carry):
            for i, x in enumerate(read(step)):
                across = slice(i * TILE, (i + 1) * TILE)
                value, slope = gelu_pair(dot(x, w_own(i, 0), 1, 0))
                active = value.astype(jnp.bfloat16)
                delta = dot(active, w_own(i, 1), 1, 0)
                cotangent = (loss_scale * (x.astype(jnp.float32) + delta)).astype(jnp.bfloat16)
                grad_act = dot(cotangent, w_own(i, 1), 1, 1)
                grad_pre = (grad_act * slope).astype(jnp.bfloat16)
                first_sum[across, :] += dot(x, grad_pre, 0, 0)
                second_sum[:, across] += dot(active, cotangent, 0, 0)
            return carry

        lax.fori_loop(0, steps, go, 0, unroll=min(steps, 4))

    for i in range(2):
        across = slice(i * TILE, (i + 1) * TILE)
        for copy in range(out_ref.shape[0]):
            out_ref[copy, i, 0] = first_sum[across, :].astype(out_ref.dtype)
            out_ref[copy, i, 1] = second_sum[:, across].astype(out_ref.dtype)


def unit_grads(blocks, weights, order, flags, per_half, owners, copies, loss_scale):
    sources, _, rows, _ = blocks.shape
    smem = pl.BlockSpec(memory_space=pltpu.SMEM)
    vmem = pl.BlockSpec(memory_space=pltpu.VMEM)
    return pl.pallas_call(
        functools.partial(grads_kernel, per_half, owners, loss_scale),
        out_shape=jax.ShapeDtypeStruct((copies, 2, 2, TILE, TILE), jnp.bfloat16),
        in_specs=[smem, smem, vmem, vmem],
        out_specs=vmem,
        scratch_shapes=[
            pltpu.VMEM((2 * TILE, TILE), jnp.float32),
            pltpu.VMEM((TILE, 2 * TILE), jnp.float32),
        ],
        compiler_params=IN_VMEM,
        cost_estimate=pl.CostEstimate(
            flops=20 * sources * rows * TILE * TILE,
            bytes_accessed=4 * sources * rows * TILE,
            transcendentals=2 * sources * rows * TILE,
        ),
    )(order, flags, blocks, weights)


def place_kernel(per_half, order_ref, counts_ref, same_ref, other_ref, out_ref, zeros, sems, zero_sems):
    owner, owners = lax.axis_index("fsdp"), counts_ref.shape[2]
    per_owner = out_ref.shape[0]
    zeros[...] = jnp.zeros_like(zeros)

    def each(act):
        for i in range(4 * per_half):
            at = order_ref[i] - owner * per_owner
            mine = (at >= 0) & (at < per_owner)
            place = unit_place(i // 2, per_half, owners)
            near = owner % CORES == place % CORES
            for grads_ref, where in ((same_ref, near), (other_ref, jnp.logical_not(near))):

                @pl.when(mine & where)
                def _():
                    act(
                        pltpu.make_async_copy(
                            grads_ref.at[place // CORES, i % 2], out_ref.at[at], sems.at[i]
                        )
                    )

        for slot in range(per_owner):

            @pl.when(counts_ref[0, 0, owner] <= slot)
            def _():
                act(pltpu.make_async_copy(zeros, out_ref.at[slot], zero_sems.at[slot]))

    each(lambda copy: copy.start())
    each(lambda copy: copy.wait())


def place(same, other, order, counts, per_half, per_owner):
    smem = pl.BlockSpec(memory_space=pltpu.SMEM)
    hbm = pl.BlockSpec(memory_space=pl.ANY)
    return pl.pallas_call(
        functools.partial(place_kernel, per_half),
        out_shape=jax.ShapeDtypeStruct((per_owner,) + same.shape[2:], same.dtype),
        in_specs=[smem, smem, hbm, hbm],
        out_specs=hbm,
        scratch_shapes=[
            pltpu.VMEM(same.shape[2:], same.dtype),
            pltpu.SemaphoreType.DMA((4 * per_half,)),
            pltpu.SemaphoreType.DMA((per_owner,)),
        ],
        compiler_params=IN_VMEM,
        cost_estimate=pl.CostEstimate(flops=0, bytes_accessed=1_000_000, transcendentals=0),
    )(order, counts, same, other)


def body(x_down, x_up, w_tiles, tile_rows, tile_cols, counts):
    rows_here = x_down.shape[2]
    slots, owners = tile_cols.shape[2], counts.shape[2]
    per_half = (live_total(slots, owners) // 2 + 1) // 2
    places = lax.axis_size("dp") * lax.axis_size("fsdp")
    sections = lax.axis_size("section")
    halfway = sections // 2
    loss_scale = float(2 * rows_here * places) ** (-0.5)

    packed, own_w, far_w, order, flags = pack(
        x_down, x_up, w_tiles, tile_rows, tile_cols, counts, per_half, places, halfway
    )
    groups = [
        [(s + side * halfway) * places + place for side in range(2) for place in range(places)]
        for s in range(halfway)
    ]
    blocks = lax.all_to_all(
        packed, ("section",) + PLANE, split_axis=0, concat_axis=0,
        axis_index_groups=groups, tiled=True,
    )
    weights = share_weights(own_w, far_w)
    copies = places // CORES
    mine = unit_grads(blocks, weights, order, flags, per_half, owners, copies, loss_scale)
    same_core = [
        [place for place in range(places) if place % CORES == core] for core in range(CORES)
    ]
    same = lax.all_to_all(
        mine, PLANE, split_axis=0, concat_axis=0, axis_index_groups=same_core, tiled=True
    )
    other = swapped(same, 1)
    return place(same, other, order, counts, per_half, slots // owners)[None]


def solution(mesh):
    in_specs = (
        P("section", "dp", "fsdp", None),
        P("section", "dp", "fsdp", None),
        P("section", None, "fsdp", None, None, None),
        P("section", None, None),
        P("section", None, None),
        P("section", None, None),
    )
    out_specs = P("section", "fsdp", None, None, None)
    return jax.shard_map(body, mesh=mesh, in_specs=in_specs, out_specs=out_specs, check_vma=False)
```

profile of v0, /device:TPU:0, one launch (start us, length us, event | category | flops | bytes accessed | tf_op | source)
XLA Modules:
  0.0 58.6 jit_solution(5997796922352506672)
XLA Ops:
  0.0 4.4 %shard_map.64 = (bf16[16,2,128,128]{3,2,1,0:T(8,128)(2,1)}, bf16[5,2,128,128]{3,2,1,0:T(8,128)(2,1)}, bf16[2,2,128,128]{3,2,1,0:T(8,128)(2,1)}, s32[18]{0:T(128)}, s32[18]{0:T(128)}) custom-call(s32[1,2,20]{2,1,0:T(2,128)} %rows_ref.1, s32[1,2,20]{2,1,0:T(2,128)} %cols_ref.1, s32[1,2,4]{2,1,0:T(2,128)} %counts_ref.3, bf16[1,1,128,6144]{3,2,1,0:T(8,128)(2,1)} %down_ref.1, ...), custom_call_target="tpu_custom_call" | custom-call | bytes 2097152 | tf_op jit(solution)/shard_map/pallas_call | solution.py:151
  4.4 0.0 copy-start.4
  4.4 0.0 copy-start.3
  4.4 7.4 %all-to-all-start = ((bf16[16,2,128,128]{3,2,1,0:T(8,128)(2,1)}), bf16[16,2,128,128]{3,2,1,0:T(8,128)(2,1)S(1)}, u32[]{:S(2)}, u32[]{:S(2)}) async-start(bf16[16,2,128,128]{3,2,1,0:T(8,128)(2,1)} %get-tuple-element.12), calls=%async_computation | async-start | bytes 2097152 | tf_op jit(solution)/shard_map/all_to_all | solution.py:348
  11.8 0.0 copy-start.1
  11.8 0.0 copy-start.2
  11.9 0.0 copy-done.4
  11.9 2.0 %collective-permute-start = (bf16[2,2,128,128]{3,2,1,0:T(8,128)(2,1)S(1)}, bf16[2,2,128,128]{3,2,1,0:T(8,128)(2,1)S(1)}, u32[]{:S(2)}, u32[]{:S(2)}) collective-permute-start(bf16[2,2,128,128]{3,2,1,0:T(8,128)(2,1)S(1)} %copy-done.4), channel_id=1, source_target_pairs={{0,2},{1,3},{2,0},{3,1},{4,6},{5,7},{6,4},{7,5},{8,10},{9,11},{10,... | collective-permute-start | bytes 393224 | tf_op jit(solution)/shard_map/ppermute | solution.py:178
  13.9 10.7 %collective-permute-done = bf16[2,2,128,128]{3,2,1,0:T(8,128)(2,1)S(1)} collective-permute-done((bf16[2,2,128,128]{3,2,1,0:T(8,128)(2,1)S(1)}, bf16[2,2,128,128]{3,2,1,0:T(8,128)(2,1)S(1)}, u32[]{:S(2)}, u32[]{:S(2)}) %collective-permute-start) | collective-permute-done | bytes 131104 | tf_op jit(solution)/shard_map/ppermute | solution.py:178
  24.5 0.0 copy-done.3
  24.6 0.1 collective-permute-start.1
  24.7 1.8 %collective-permute-done.1 = bf16[7,2,128,128]{3,2,1,0:T(8,128)(2,1)S(1)} collective-permute-done((bf16[7,2,128,128]{3,2,1,0:T(8,128)(2,1)S(1)}, bf16[7,2,128,128]{3,2,1,0:T(8,128)(2,1)S(1)}, u32[]{:S(2)}, u32[]{:S(2)}) %collective-permute-start.1) | collective-permute-done | bytes 458784 | tf_op jit(solution)/shard_map/ppermute | solution.py:178
  26.5 0.1 pad_maximum_fusion.w_ref
  26.6 13.6 %all-to-all-done.x_ref = bf16[16,2,128,128]{3,2,1,0:T(8,128)(2,1)S(1)} async-done(((bf16[16,2,128,128]{3,2,1,0:T(8,128)(2,1)}), bf16[16,2,128,128]{3,2,1,0:T(8,128)(2,1)S(1)}, u32[]{:S(2)}, u32[]{:S(2)}) %all-to-all-start) | async-done | bytes 1048608 | tf_op jit(solution)/shard_map/all_to_all | solution.py:348
  40.1 0.0 copy-done.1
  40.1 0.0 copy-done.2
  40.1 0.0 copy-start
  40.1 4.0 %shard_map.65 = bf16[4,2,2,128,128]{4,3,2,1,0:T(8,128)(2,1)S(1)} custom-call(s32[18]{0:T(128)S(1)} %copy-done.1, s32[18]{0:T(128)S(1)} %copy-done.2, bf16[16,2,128,128]{3,2,1,0:T(8,128)(2,1)S(1)} %all-to-all-done.x_ref, bf16[14,2,128,128]{3,2,1,0:T(8,128)(2,1)S(1)} %pad_maximum_fusion.w_ref), custom_call_target="tpu_custom_call" | custom-call | flops 671088640 | bytes 1048576 | tf_op jit(solution)/shard_map/pallas_call | solution.py:265
  44.2 11.1 %all_to_all.10.same_ref = bf16[4,2,2,128,128]{4,3,2,1,0:T(8,128)(2,1)S(1)} all-to-all(bf16[4,2,2,128,128]{4,3,2,1,0:T(8,128)(2,1)S(1)} %shard_map.65), channel_id=1, replica_groups={{0,2,4,6},{1,3,5,7},{8,10,12,14},{9,11,13,15},{16,18,20,22},{17,19,21,2..., dimensions={0} | all-to-all | bytes 1048576 | tf_op jit(solution)/shard_map/all_to_all | solution.py:358
  55.2 0.0 collective-permute-start.2
  55.2 1.9 %collective-permute-done.2.other_ref = bf16[4,2,2,128,128]{4,3,2,1,0:T(8,128)(2,1)S(1)} collective-permute-done((bf16[4,2,2,128,128]{4,3,2,1,0:T(8,128)(2,1)S(1)}, bf16[4,2,2,128,128]{4,3,2,1,0:T(8,128)(2,1)S(1)}, u32[]{:S(2)}, u32[]{:S(2)}) %collective-permute-start.2) | collective-permute-done | bytes 524320 | tf_op jit(solution)/shard_map/ppermute | solution.py:178
  57.1 0.0 copy-done
  57.1 1.5 %shard_map.66 = bf16[5,2,128,128]{3,2,1,0:T(8,128)(2,1)} custom-call(s32[18]{0:T(128)S(1)} %copy-done.1, s32[1,2,4]{2,1,0:T(2,128)S(1)} %copy-done, bf16[4,2,2,128,128]{4,3,2,1,0:T(8,128)(2,1)S(1)} %all_to_all.10.same_ref, bf16[4,2,2,128,128]{4,3,2,1,0:T(8,128)(2,1)S(1)} %collective-permute-done.2.other_ref), custom_call_target="tpu_custom_call" | custom-call | bytes 1000000 | tf_op jit(solution)/shard_map/pallas_call | solution.py:317
  (1 shorter events, 0.0 us)
Async XLA Ops:
  4.4 7.5 %copy-start.4 = (bf16[2,2,128,128]{3,2,1,0:T(8,128)(2,1)S(1)}, bf16[2,2,128,128]{3,2,1,0:T(8,128)(2,1)}, u32[]{:S(2)}) copy-start(bf16[2,2,128,128]{3,2,1,0:T(8,128)(2,1)} %get-tuple-element.14) | copy-start | bytes 393220
  4.4 20.2 %copy-start.3 = (bf16[5,2,128,128]{3,2,1,0:T(8,128)(2,1)S(1)}, bf16[5,2,128,128]{3,2,1,0:T(8,128)(2,1)}, u32[]{:S(2)}) copy-start(bf16[5,2,128,128]{3,2,1,0:T(8,128)(2,1)} %get-tuple-element.13) | copy-start | bytes 983044
  4.4 35.8 %all-to-all-start = ((bf16[16,2,128,128]{3,2,1,0:T(8,128)(2,1)}), bf16[16,2,128,128]{3,2,1,0:T(8,128)(2,1)S(1)}, u32[]{:S(2)}, u32[]{:S(2)}) async-start(bf16[16,2,128,128]{3,2,1,0:T(8,128)(2,1)} %get-tuple-element.12), calls=%async_computation | async-start | bytes 2097152 | tf_op jit(solution)/shard_map/all_to_all | solution.py:348
  11.8 28.3 %copy-start.1 = (s32[18]{0:T(128)S(1)}, s32[18]{0:T(128)}, u32[]{:S(2)}) copy-start(s32[18]{0:T(128)} %get-tuple-element.10.order_ref) | copy-start | bytes 220
  11.8 28.3 %copy-start.2 = (s32[18]{0:T(128)S(1)}, s32[18]{0:T(128)}, u32[]{:S(2)}) copy-start(s32[18]{0:T(128)} %get-tuple-element.11.flags_ref) | copy-start | bytes 220
  11.9 12.7 %collective-permute-start = (bf16[2,2,128,128]{3,2,1,0:T(8,128)(2,1)S(1)}, bf16[2,2,128,128]{3,2,1,0:T(8,128)(2,1)S(1)}, u32[]{:S(2)}, u32[]{:S(2)}) collective-permute-start(bf16[2,2,128,128]{3,2,1,0:T(8,128)(2,1)S(1)} %copy-done.4), channel_id=1, source_target_pairs={{0,2},{1,3},{2,0},{3,1},{4,6},{5,7},{6,4},{7,5},{8,10},{9,11},{10,... | collective-permute-start | bytes 393224 | tf_op jit(solution)/shard_map/ppermute | solution.py:178
  24.6 1.9 %collective-permute-start.1 = (bf16[7,2,128,128]{3,2,1,0:T(8,128)(2,1)S(1)}, bf16[7,2,128,128]{3,2,1,0:T(8,128)(2,1)S(1)}, u32[]{:S(2)}, u32[]{:S(2)}) collective-permute-start(bf16[7,2,128,128]{3,2,1,0:T(8,128)(2,1)S(1)} %pad_maximum_fusion.1), channel_id=1, source_target_pairs={{0,1},{1,0},{2,3},{3,2},{4,5},{5,4},{6,7},{7,6},{8,9},{9,8},{10,11... | collective-permute-start | bytes 1376264 | tf_op jit(solution)/shard_map/ppermute | solution.py:178
  40.1 17.0 %copy-start = (s32[1,2,4]{2,1,0:T(2,128)S(1)}, s32[1,2,4]{2,1,0:T(2,128)}, u32[]{:S(2)}) copy-start(s32[1,2,4]{2,1,0:T(2,128)} %counts_ref.3) | copy-start | bytes 100
  55.2 1.9 %collective-permute-start.2 = (bf16[4,2,2,128,128]{4,3,2,1,0:T(8,128)(2,1)S(1)}, bf16[4,2,2,128,128]{4,3,2,1,0:T(8,128)(2,1)S(1)}, u32[]{:S(2)}, u32[]{:S(2)}) collective-permute-start(bf16[4,2,2,128,128]{4,3,2,1,0:T(8,128)(2,1)S(1)} %all_to_all.10.same_ref), channel_id=1, source_target_pairs={{0,1},{1,0},{2,3},{3,2},{4,5},{5,4},{6,7},{7,6},{8,9},{9,8},{10,11... | collective-permute-start | bytes 1572872 | tf_op jit(solution)/shard_map/ppermute | solution.py:178
where the time goes:
time: 58.9 us; the launch traced here: 58.6 us
  waiting for transfers between devices  28 us (48%)
  blocking collectives  11.1 us (19%)
  Pallas kernels  9.84 us (17%)
  starting transfers between devices  9.51 us (16%)
    ppermute x3, waiting for transfers between devices, swapped(): return lax.ppermute(array, 'fsdp', [(i, i ^ apart) for i in range(size)])  14.4 us
    all_to_all x1, waiting for transfers between devices, body(): lax.all_to_all(packed, ('section',) + PLANE, split_axis=0, concat_axis=0,...  13.6 us
    all_to_all x1, blocking collectives, body(): lax.all_to_all(mine, PLANE, split_axis=0, concat_axis=0, axis_index_group...  11.1 us
    all_to_all x1, starting transfers between devices, body(): lax.all_to_all(packed, ('section',) + PLANE, split_axis=0, concat_axis=0,...  7.44 us
    pallas_call x1, Pallas kernels, pack(): pl.pallas_call(functools.partial(pack_kernel, per_half, halfway), out_sha...  4.35 us
    pallas_call x1, Pallas kernels, unit_grads(): pl.pallas_call(functools.partial(grads_kernel, per_half, owners, loss_sca...  4 us
    ppermute x3, starting transfers between devices, swapped(): return lax.ppermute(array, 'fsdp', [(i, i ^ apart) for i in range(size)])  2.06 us
    pallas_call x1, Pallas kernels, place(): pl.pallas_call(functools.partial(place_kernel, per_half), out_shape=jax.S...  1.49 us
  transfers between devices with their start and end apart: 4, of which 4 were waited for; matrix products, arithmetic and copies ran while one was open for 0% of the time, Pallas kernels for 0%

commit v1 on v0

--- a/solution.py
+++ b/solution.py
@@ -50,9 +50,9 @@
     cols_ref, counts_ref, which, slots, per_half, order_ref, flags_ref, first_ref, last_ref
 ):
     per_owner, middle, unused = slots // counts_ref.shape[2], slots // 2, 4 * per_half
-    for i in range(order_ref.shape[0]):
-        order_ref[i] = -1
-        flags_ref[i] = 0
+    for i in range(order_ref.shape[1]):
+        order_ref[which, i] = -1
+        flags_ref[which, i] = 0
     cols = []
     for s in range(slots):
         living = counts_ref[0, which, s // per_owner] > s % per_owner
@@ -64,9 +64,9 @@
 
     def put(unit, slot_a, slot_b, coupled, really):
         at = jnp.where(really, 2 * unit, unused)
-        order_ref[at] = slot_a
-        order_ref[at + 1] = slot_b
-        flags_ref[at] = coupled
+        order_ref[which, at] = slot_a
+        order_ref[which, at + 1] = slot_b
+        flags_ref[which, at] = coupled
 
     count = lambda condition: jnp.where(condition, 1, 0)
     alone, mixed = [], []
@@ -99,73 +99,55 @@
 
 
 def pack_kernel(
-    per_half, halfway, rows_ref, cols_ref, counts_ref, down_ref, up_ref, w_ref,
-    out_ref, own_w_ref, far_w_ref, order_ref, flags_ref,
-    up_order_ref, up_flags_ref, first_ref, last_ref, sems, w_sems,
+    per_half, rows_ref, cols_ref, counts_ref, down_ref, up_ref, w_ref,
+    out_ref, own_w_ref, order_ref, flags_ref, first_ref, last_ref, sems, w_sem,
 ):
     slots, owners = cols_ref.shape[2], counts_ref.shape[2]
-    per_owner, places, units = slots // owners, out_ref.shape[0] // 2, 2 * per_half
-    behind = jnp.where(lax.axis_index("section") < halfway, 0, places)
-    copies = [pltpu.make_async_copy(w_ref.at[0, 0], own_w_ref, w_sems.at[CORES])]
+    places, units = out_ref.shape[0], 2 * per_half
+    copies = [pltpu.make_async_copy(w_ref.at[0], own_w_ref, w_sem)]
     copies[0].start()
     used = [unit_place(unit, per_half, owners) for unit in range(units)]
-    for which, x_ref, order, flags, base in (
-        (1, up_ref, up_order_ref, up_flags_ref, places - behind),
-        (0, down_ref, order_ref, flags_ref, behind),
-    ):
+    for which, x_ref in ((1, up_ref), (0, down_ref)):
         order_units(
-            cols_ref, counts_ref, which, slots, per_half, order, flags, first_ref, last_ref
+            cols_ref, counts_ref, which, slots, per_half, order_ref, flags_ref, first_ref, last_ref
         )
         for i in range(2 * units):
-            row = rows_ref[0, which, jnp.maximum(order[i], 0)]
+            row = rows_ref[0, which, jnp.maximum(order_ref[which, i], 0)]
             at = pl.multiple_of(row * TILE, TILE)
             copy = pltpu.make_async_copy(
                 x_ref.at[0, 0, :, pl.ds(at, TILE)],
-                out_ref.at[base + used[i // 2], i % 2],
-                sems.at[2 * units * which + i],
+                out_ref.at[used[i // 2], which, i % 2],
+                sems.at[which, i],
             )
             copy.start()
             copies.append(copy)
-    owner = lax.axis_index("fsdp")
-    for core in range(CORES):
-        at = jnp.minimum(lax.axis_index("dp") * CORES + core, per_half - 1)
-        asker = (1 - owner // CORES) * per_half + at
-        held = order_ref[2 * asker + 1] - owner * per_owner
-        held = jnp.where((held >= 0) & (held < per_owner), held, 0)
-        copy = pltpu.make_async_copy(w_ref.at[0, 0, held], far_w_ref.at[core], w_sems.at[core])
-        copy.start()
-        copies.append(copy)
     for place in range(places):
         if place not in used:
             out_ref[place] = jnp.zeros(out_ref.shape[1:], out_ref.dtype)
-            out_ref[places + place] = jnp.zeros(out_ref.shape[1:], out_ref.dtype)
     for copy in copies:
         copy.wait()
 
 
-def pack(x_down, x_up, w_tiles, tile_rows, tile_cols, counts, per_half, places, halfway):
+def pack(x_down, x_up, w_tiles, tile_rows, tile_cols, counts, per_half, places):
     rows, units = x_down.shape[2], 2 * per_half
     smem = pl.BlockSpec(memory_space=pltpu.SMEM)
     vmem = pl.BlockSpec(memory_space=pltpu.VMEM)
     hbm = pl.BlockSpec(memory_space=pl.ANY)
     return pl.pallas_call(
-        functools.partial(pack_kernel, per_half, halfway),
+        functools.partial(pack_kernel, per_half),
         out_shape=[
-            jax.ShapeDtypeStruct((2 * places, 2, rows, TILE), x_down.dtype),
-            jax.ShapeDtypeStruct(w_tiles.shape[2:], w_tiles.dtype),
-            jax.ShapeDtypeStruct((CORES,) + w_tiles.shape[3:], w_tiles.dtype),
-            jax.ShapeDtypeStruct((2 * units + 2,), jnp.int32),
-            jax.ShapeDtypeStruct((2 * units + 2,), jnp.int32),
+            jax.ShapeDtypeStruct((places, 2, 2, rows, TILE), x_down.dtype),
+            jax.ShapeDtypeStruct(w_tiles.shape[1:], w_tiles.dtype),
+            jax.ShapeDtypeStruct((2, 2 * units + 2), jnp.int32),
+            jax.ShapeDtypeStruct((2, 2 * units + 2), jnp.int32),
         ],
         in_specs=[smem, smem, smem, hbm, hbm, hbm],
-        out_specs=[vmem, vmem, vmem, smem, smem],
+        out_specs=[vmem, vmem, smem, smem],
         scratch_shapes=[
-            pltpu.SMEM((2 * units + 2,), jnp.int32),
-            pltpu.SMEM((2 * units + 2,), jnp.int32),
             pltpu.SMEM((COLUMNS + 1,), jnp.int32),
             pltpu.SMEM((COLUMNS + 1,), jnp.int32),
-            pltpu.SemaphoreType.DMA((4 * units,)),
-            pltpu.SemaphoreType.DMA((CORES + 1,)),
+            pltpu.SemaphoreType.DMA((2, 2 * units)),
+            pltpu.SemaphoreType.DMA,
         ],
         cost_estimate=pl.CostEstimate(
             flops=0, bytes_accessed=16 * units * rows * TILE, transcendentals=0
@@ -178,15 +160,31 @@
     return lax.ppermute(array, "fsdp", [(i, i ^ apart) for i in range(size)])
 
 
-def share_weights(own_w, far_w):
-    both = jnp.concatenate([own_w, swapped(far_w, CORES)], axis=0)
-    return jnp.concatenate([both, swapped(both, 1)], axis=0)
-
-
-def weights_at(slot, per_owner):
-    me, owner = lax.axis_index("fsdp"), slot // per_owner
-    here = jnp.where(owner // CORES == me // CORES, slot - owner * per_owner, per_owner + me % CORES)
-    return here + jnp.where(owner % CORES == me % CORES, 0, per_owner + CORES)
+def near_at(slot, per_owner):
+    owner = slot // per_owner
+    other = jnp.where(owner % CORES == lax.axis_index("fsdp") % CORES, 0, per_owner)
+    return other + slot - owner * per_owner
+
+
+def far_kernel(per_half, order_ref, near_ref, out_ref):
+    per_owner, owners = near_ref.shape[1] // CORES, 2 * CORES
+    unit = unit_here(per_half, owners)
+    asker = jnp.where(unit < per_half, unit + per_half, unit - per_half)
+    for which in range(2):
+        slot = jnp.maximum(order_ref[which, 2 * asker + 1], 0)
+        out_ref[which] = near_ref[which, near_at(slot, per_owner)]
+
+
+def far_weights(near, order, per_half):
+    vmem = pl.BlockSpec(memory_space=pltpu.VMEM)
+    return pl.pallas_call(
+        functools.partial(far_kernel, per_half),
+        out_shape=jax.ShapeDtypeStruct(near.shape[:1] + near.shape[2:], near.dtype),
+        in_specs=[pl.BlockSpec(memory_space=pltpu.SMEM), vmem],
+        out_specs=vmem,
+        compiler_params=IN_VMEM,
+        cost_estimate=pl.CostEstimate(flops=0, bytes_accessed=300_000, transcendentals=0),
+    )(order, near)
 
 
 def dot(a, b, over_a, over_b):
@@ -196,32 +194,43 @@
 
 
 def grads_kernel(
-    per_half, owners, loss_scale, order_ref, flags_ref, x_ref, w_ref, out_ref,
-    first_sum, second_sum,
+    which, per_half, owners, loss_scale, order_ref, flags_ref, x_ref, near_ref, far_ref, out_ref,
+    w_unit, first_sum, second_sum,
 ):
-    sources, _, rows, _ = x_ref.shape
-    per_owner = w_ref.shape[0] // 2 - CORES
+    sources, _, _, rows, _ = x_ref.shape
+    per_owner = near_ref.shape[1] // CORES
     unit = unit_here(per_half, owners)
-    ats = [weights_at(jnp.maximum(order_ref[2 * unit + i], 0), per_owner) for i in range(2)]
-    w_own = lambda i, k: w_ref[ats[i], k]
+    half = lax.axis_index("fsdp") // CORES
+    for i in range(2):
+        slot = jnp.maximum(order_ref[which, 2 * unit + i], 0)
+        near = slot // per_owner // CORES == half
+
+        @pl.when(near)
+        def _():
+            w_unit[i] = near_ref[which, near_at(slot, per_owner)]
+
+        @pl.when(jnp.logical_not(near))
+        def _():
+            w_unit[i] = far_ref[which]
+
     first_sum[...] = jnp.zeros_like(first_sum)
     second_sum[...] = jnp.zeros_like(second_sum)
     together = min(SOURCES_AT_ONCE, sources)
     steps = sources // together
-    coupled = flags_ref[2 * unit] == 1
+    coupled = flags_ref[which, 2 * unit] == 1
 
     def read(step):
         at = step * together
         return [
-            x_ref[pl.ds(at, together), i].reshape(together * rows, TILE) for i in range(2)
+            x_ref[pl.ds(at, together), which, i].reshape(together * rows, TILE) for i in range(2)
         ]
 
     @pl.when(coupled)
     def _():
         def go(step, carry):
             xs = jnp.concatenate(read(step), axis=1)
-            firsts = jnp.concatenate([w_own(0, 0), w_own(1, 0)], axis=0)
-            seconds = jnp.concatenate([w_own(0, 1), w_own(1, 1)], axis=1)
+            firsts = jnp.concatenate([w_unit[0, 0], w_unit[1, 0]], axis=0)
+            seconds = jnp.concatenate([w_unit[0, 1], w_unit[1, 1]], axis=1)
             value, slope = gelu_pair(dot(xs, firsts, 1, 0))
             active = value.astype(jnp.bfloat16)
             delta = dot(active, seconds, 1, 0)
@@ -239,11 +248,11 @@
         def go(step, carry):
             for i, x in enumerate(read(step)):
                 across = slice(i * TILE, (i + 1) * TILE)
-                value, slope = gelu_pair(dot(x, w_own(i, 0), 1, 0))
+                value, slope = gelu_pair(dot(x, w_unit[i, 0], 1, 0))
                 active = value.astype(jnp.bfloat16)
-                delta = dot(active, w_own(i, 1), 1, 0)
+                delta = dot(active, w_unit[i, 1], 1, 0)
                 cotangent = (loss_scale * (x.astype(jnp.float32) + delta)).astype(jnp.bfloat16)
-                grad_act = dot(cotangent, w_own(i, 1), 1, 1)
+                grad_act = dot(cotangent, w_unit[i, 1], 1, 1)
                 grad_pre = (grad_act * slope).astype(jnp.bfloat16)
                 first_sum[across, :] += dot(x, grad_pre, 0, 0)
                 second_sum[:, across] += dot(active, cotangent, 0, 0)
@@ -253,21 +262,21 @@
 
     for i in range(2):
         across = slice(i * TILE, (i + 1) * TILE)
-        for copy in range(out_ref.shape[0]):
-            out_ref[copy, i, 0] = first_sum[across, :].astype(out_ref.dtype)
-            out_ref[copy, i, 1] = second_sum[:, across].astype(out_ref.dtype)
-
-
-def unit_grads(blocks, weights, order, flags, per_half, owners, copies, loss_scale):
-    sources, _, rows, _ = blocks.shape
+        out_ref[i, 0] = first_sum[across, :].astype(out_ref.dtype)
+        out_ref[i, 1] = second_sum[:, across].astype(out_ref.dtype)
+
+
+def unit_grads(which, blocks, near, far, order, flags, per_half, owners, loss_scale, dtype):
+    sources, _, _, rows, _ = blocks.shape
     smem = pl.BlockSpec(memory_space=pltpu.SMEM)
     vmem = pl.BlockSpec(memory_space=pltpu.VMEM)
     return pl.pallas_call(
-        functools.partial(grads_kernel, per_half, owners, loss_scale),
-        out_shape=jax.ShapeDtypeStruct((copies, 2, 2, TILE, TILE), jnp.bfloat16),
-        in_specs=[smem, smem, vmem, vmem],
+        functools.partial(grads_kernel, which, per_half, owners, loss_scale),
+        out_shape=jax.ShapeDtypeStruct((2, 2, TILE, TILE), dtype),
+        in_specs=[smem, smem, vmem, vmem, vmem],
         out_specs=vmem,
         scratch_shapes=[
+            pltpu.VMEM((2, 2, TILE, TILE), jnp.bfloat16),
             pltpu.VMEM((2 * TILE, TILE), jnp.float32),
             pltpu.VMEM((TILE, 2 * TILE), jnp.float32),
         ],
@@ -277,7 +286,25 @@
             bytes_accessed=4 * sources * rows * TILE,
             transcendentals=2 * sources * rows * TILE,
         ),
-    )(order, flags, blocks, weights)
+    )(order, flags, blocks, near, far)
+
+
+def add_kernel(own_ref, arrived_ref, out_ref):
+    total = (own_ref[...] + arrived_ref[...].astype(jnp.float32)).astype(out_ref.dtype)
+    for copy in range(out_ref.shape[0]):
+        out_ref[copy] = total
+
+
+def add(own, arrived, copies):
+    vmem = pl.BlockSpec(memory_space=pltpu.VMEM)
+    return pl.pallas_call(
+        add_kernel,
+        out_shape=jax.ShapeDtypeStruct((copies,) + own.shape, jnp.bfloat16),
+        in_specs=[vmem, vmem],
+        out_specs=vmem,
+        compiler_params=IN_VMEM,
+        cost_estimate=pl.CostEstimate(flops=own.size, bytes_accessed=900_000, transcendentals=0),
+    )(own, arrived)
 
 
 def place_kernel(per_half, order_ref, counts_ref, same_ref, other_ref, out_ref, zeros, sems, zero_sems):
@@ -287,7 +314,7 @@
 
     def each(act):
         for i in range(4 * per_half):
-            at = order_ref[i] - owner * per_owner
+            at = order_ref[0, i] - owner * per_owner
             mine = (at >= 0) & (at < per_owner)
             place = unit_place(i // 2, per_half, owners)
             near = owner % CORES == place % CORES
@@ -335,23 +362,21 @@
     per_half = (live_total(slots, owners) // 2 + 1) // 2
     places = lax.axis_size("dp") * lax.axis_size("fsdp")
     sections = lax.axis_size("section")
-    halfway = sections // 2
+    across = [(i, (i + sections // 2) % sections) for i in range(sections)]
     loss_scale = float(2 * rows_here * places) ** (-0.5)
 
-    packed, own_w, far_w, order, flags = pack(
-        x_down, x_up, w_tiles, tile_rows, tile_cols, counts, per_half, places, halfway
-    )
-    groups = [
-        [(s + side * halfway) * places + place for side in range(2) for place in range(places)]
-        for s in range(halfway)
-    ]
-    blocks = lax.all_to_all(
-        packed, ("section",) + PLANE, split_axis=0, concat_axis=0,
-        axis_index_groups=groups, tiled=True,
-    )
-    weights = share_weights(own_w, far_w)
-    copies = places // CORES
-    mine = unit_grads(blocks, weights, order, flags, per_half, owners, copies, loss_scale)
+    packed, own_w, order, flags = pack(
+        x_down, x_up, w_tiles, tile_rows, tile_cols, counts, per_half, places
+    )
+    blocks = lax.all_to_all(packed, PLANE, split_axis=0, concat_axis=0, tiled=True)
+    near = jnp.concatenate([own_w, swapped(own_w, 1)], axis=1)
+    far = swapped(far_weights(near, order, per_half), CORES)
+    grads = functools.partial(
+        unit_grads, blocks=blocks, near=near, far=far, order=order, flags=flags,
+        per_half=per_half, owners=owners, loss_scale=loss_scale,
+    )
+    arrived = lax.ppermute(grads(1, dtype=jnp.bfloat16), "section", across)
+    mine = add(grads(0, dtype=jnp.float32), arrived, places // CORES)
     same_core = [
         [place for place in range(places) if place % CORES == core] for core in range(CORES)
     ]

time: 58.9 us -> 53.1 us (0.902)
  waiting for transfers between devices: 28 us -> 19.1 us
  Pallas kernels: 9.84 us -> 11.5 us
  starting transfers between devices: 9.51 us -> 10.9 us
    all_to_all x1, waiting for transfers between devices: 13.6 us -> 0.01 us  [body(): lax.all_to_all(packed, PLANE, split_axis=0, concat_axis=0, tiled=True)]
    ppermute x0 -> x1, waiting for transfers between devices: none -> 3.2 us  [body(): arrived = lax.ppermute(grads(1, dtype=jnp.bfloat16), 'section', across)]
    ppermute x0 -> x1, starting transfers between devices: none -> 3.1 us  [body(): arrived = lax.ppermute(grads(1, dtype=jnp.bfloat16), 'section', across)]
    all_to_all x1, starting transfers between devices: 7.44 us -> 5.31 us  [body(): lax.all_to_all(packed, PLANE, split_axis=0, concat_axis=0, tiled=True)]
    pallas_call x2 -> x5, Pallas kernels: 8.35 us -> 9.96 us  [the longest x1 4.76 us: pack(): pl.pallas_call(functools.partial(pack_kernel, per_half), out_shape=[jax.S...]
    ppermute x3, waiting for transfers between devices: 14.4 us -> 15.9 us  [swapped(): return lax.ppermute(array, 'fsdp', [(i, i ^ apart) for i in range(size)])]
  transfers between devices with their start and end apart: 4 -> 5, of which waited for: 4 -> 4; matrix products, arithmetic and copies ran while one was open for 0% -> 0% of each run, Pallas kernels for 0% -> 6%
where the time goes in v1:
time: 53.1 us; the launch traced here: 52.9 us
  waiting for transfers between devices  19.1 us (36%)
  Pallas kernels  11.5 us (22%)
  blocking collectives  11.2 us (21%)
  starting transfers between devices  10.9 us (21%)
    ppermute x3, waiting for transfers between devices, swapped(): return lax.ppermute(array, 'fsdp', [(i, i ^ apart) for i in range(size)])  15.9 us
    all_to_all x1, blocking collectives, body(): lax.all_to_all(mine, PLANE, split_axis=0, concat_axis=0, axis_index_group...  11.2 us
    all_to_all x1, starting transfers between devices, body(): lax.all_to_all(packed, PLANE, split_axis=0, concat_axis=0, tiled=True)  5.31 us
    pallas_call x1, Pallas kernels, pack(): pl.pallas_call(functools.partial(pack_kernel, per_half), out_shape=[jax.S...  4.76 us
    pallas_call x2, Pallas kernels, unit_grads(): pl.pallas_call(functools.partial(grads_kernel, which, per_half, owners, l...  4.57 us
    ppermute x1, waiting for transfers between devices, body(): arrived = lax.ppermute(grads(1, dtype=jnp.bfloat16), 'section', across)  3.2 us
    ppermute x1, starting transfers between devices, body(): arrived = lax.ppermute(grads(1, dtype=jnp.bfloat16), 'section', across)  3.1 us
    ppermute x3, starting transfers between devices, swapped(): return lax.ppermute(array, 'fsdp', [(i, i ^ apart) for i in range(size)])  2.51 us
  transfers between devices with their start and end apart: 5, of which 4 were waited for; matrix products, arithmetic and copies ran while one was open for 0% of the time, Pallas kernels for 6%

profile of v1, /device:TPU:0, one launch (start us, length us, event | category | flops | bytes accessed | tf_op | source)
XLA Modules:
  0.0 52.9 jit_solution(7607078110208643856)
XLA Ops:
  0.0 4.8 %shard_map.64 = (bf16[8,2,2,128,128]{4,3,2,1,0:T(8,128)(2,1)}, bf16[2,5,2,128,128]{4,3,2,1,0:T(8,128)(2,1)}, s32[2,18]{1,0:T(2,128)}, s32[2,18]{1,0:T(2,128)}) custom-call(s32[1,2,20]{2,1,0:T(2,128)} %rows_ref.1, s32[1,2,20]{2,1,0:T(2,128)} %cols_ref.1, s32[1,2,4]{2,1,0:T(2,128)} %counts_ref.3, bf16[1,1,128,6144]{3,2,1,0:T(8,128)(2,1)} %down_ref.1, ...), custom_call_target="tpu_custom_call" | custom-call | bytes 2097152 | tf_op jit(solution)/shard_map/pallas_call | solution.py:136
  4.8 0.0 copy-start.3
  4.8 5.3 %all-to-all-start = ((bf16[8,2,2,128,128]{4,3,2,1,0:T(8,128)(2,1)}), bf16[8,2,2,128,128]{4,3,2,1,0:T(8,128)(2,1)S(1)}, u32[]{:S(2)}, u32[]{:S(2)}) async-start(bf16[8,2,2,128,128]{4,3,2,1,0:T(8,128)(2,1)} %get-tuple-element.11), calls=%async_computation | async-start | bytes 2097152 | tf_op jit(solution)/shard_map/all_to_all | solution.py:371
  10.1 0.0 copy-done.3
  10.1 0.0 copy-start
  10.1 0.6 %collective-permute-start = (bf16[2,5,2,128,128]{4,3,2,1,0:T(8,128)(2,1)S(1)}, bf16[2,5,2,128,128]{4,3,2,1,0:T(8,128)(2,1)S(1)}, u32[]{:S(2)}, u32[]{:S(2)}) collective-permute-start(bf16[2,5,2,128,128]{4,3,2,1,0:T(8,128)(2,1)S(1)} %copy-done.3), channel_id=1, source_target_pairs={{0,1},{1,0},{2,3},{3,2},{4,5},{5,4},{6,7},{7,6},{8,9},{9,8},{10,11... | collective-permute-start | bytes 1966088 | tf_op jit(solution)/shard_map/ppermute | solution.py:160
  10.7 0.1 constant_dynamic-update-slice_fusion.1
  10.7 0.0 copy-start.1
  10.7 1.7 %collective-permute-done = bf16[2,5,2,128,128]{4,3,2,1,0:T(8,128)(2,1)S(1)} collective-permute-done((bf16[2,5,2,128,128]{4,3,2,1,0:T(8,128)(2,1)S(1)}, bf16[2,5,2,128,128]{4,3,2,1,0:T(8,128)(2,1)S(1)}, u32[]{:S(2)}, u32[]{:S(2)}) %collective-permute-start) | collective-permute-done | bytes 655392 | tf_op jit(solution)/shard_map/ppermute | solution.py:160
  12.4 0.1 constant_dynamic-update-slice_fusion.near_ref
  12.5 0.0 copy-done
  12.5 0.6 %shard_map.65 = bf16[2,2,128,128]{3,2,1,0:T(8,128)(2,1)S(1)} custom-call(s32[2,18]{1,0:T(2,128)S(1)} %copy-done, bf16[2,10,2,128,128]{4,3,2,1,0:T(8,128)(2,1)S(1)} %constant_dynamic-update-slice_fusion.near_ref), custom_call_target="tpu_custom_call" | custom-call | bytes 300000 | tf_op jit(solution)/shard_map/pallas_call | solution.py:180
  13.1 2.0 %collective-permute-start.1 = (bf16[2,2,128,128]{3,2,1,0:T(8,128)(2,1)S(1)}, bf16[2,2,128,128]{3,2,1,0:T(8,128)(2,1)S(1)}, u32[]{:S(2)}, u32[]{:S(2)}) collective-permute-start(bf16[2,2,128,128]{3,2,1,0:T(8,128)(2,1)S(1)} %shard_map.65), channel_id=1, source_target_pairs={{0,2},{1,3},{2,0},{3,1},{4,6},{5,7},{6,4},{7,5},{8,10},{9,11},{10,... | collective-permute-start | bytes 393224 | tf_op jit(solution)/shard_map/ppermute | solution.py:160
  15.1 12.3 %collective-permute-done.1.far_ref = bf16[2,2,128,128]{3,2,1,0:T(8,128)(2,1)S(1)} collective-permute-done((bf16[2,2,128,128]{3,2,1,0:T(8,128)(2,1)S(1)}, bf16[2,2,128,128]{3,2,1,0:T(8,128)(2,1)S(1)}, u32[]{:S(2)}, u32[]{:S(2)}) %collective-permute-start.1) | collective-permute-done | bytes 131104 | tf_op jit(solution)/shard_map/ppermute | solution.py:160
  27.4 0.0 all-to-all-done.x_ref
  27.4 0.0 copy-done.1
  27.4 2.1 %shard_map.67 = bf16[2,2,128,128]{3,2,1,0:T(8,128)(2,1)S(1)} custom-call(s32[2,18]{1,0:T(2,128)S(1)} %copy-done, s32[2,18]{1,0:T(2,128)S(1)} %copy-done.1, bf16[8,2,2,128,128]{4,3,2,1,0:T(8,128)(2,1)S(1)} %all-to-all-done.x_ref, bf16[2,10,2,128,128]{4,3,2,1,0:T(8,128)(2,1)S(1)} %constant_dynamic-update-slice_fusion.near_ref, ...), custom_call_target="tpu_custom_call" | custom-call | flops 335544320 | bytes 524288 | tf_op jit(solution)/shard_map/pallas_call | solution.py:273
  29.4 3.1 %collective-permute-start.2 = (bf16[2,2,128,128]{3,2,1,0:T(8,128)(2,1)S(1)}, bf16[2,2,128,128]{3,2,1,0:T(8,128)(2,1)S(1)}, u32[]{:S(2)}, u32[]{:S(2)}) collective-permute-start(bf16[2,2,128,128]{3,2,1,0:T(8,128)(2,1)S(1)} %shard_map.67), channel_id=1, source_target_pairs={{0,16},{8,24},{16,0},{24,8},{1,17},{9,25},{17,1},{25,9},{2,18},{10... | collective-permute-start | bytes 393224 | tf_op jit(solution)/shard_map/ppermute | solution.py:378
  32.5 2.5 %shard_map.66.own_ref = f32[2,2,128,128]{3,2,1,0:T(8,128)S(1)} custom-call(s32[2,18]{1,0:T(2,128)S(1)} %copy-done, s32[2,18]{1,0:T(2,128)S(1)} %copy-done.1, bf16[8,2,2,128,128]{4,3,2,1,0:T(8,128)(2,1)S(1)} %all-to-all-done.x_ref, bf16[2,10,2,128,128]{4,3,2,1,0:T(8,128)(2,1)S(1)} %constant_dynamic-update-slice_fusion.near_ref, ...), custom_call_target="tpu_custom_call" | custom-call | flops 335544320 | bytes 524288 | tf_op jit(solution)/shard_map/pallas_call | solution.py:273
  35.0 0.0 copy-start.2
  35.1 3.2 %collective-permute-done.2.arrived_ref = bf16[2,2,128,128]{3,2,1,0:T(8,128)(2,1)S(1)} collective-permute-done((bf16[2,2,128,128]{3,2,1,0:T(8,128)(2,1)S(1)}, bf16[2,2,128,128]{3,2,1,0:T(8,128)(2,1)S(1)}, u32[]{:S(2)}, u32[]{:S(2)}) %collective-permute-start.2) | collective-permute-done | bytes 131104 | tf_op jit(solution)/shard_map/ppermute | solution.py:378
  38.3 11.2 %all_to_all.10.same_ref = bf16[4,2,2,128,128]{4,3,2,1,0:T(8,128)(2,1)S(1)} all-to-all(bf16[4,2,2,128,128]{4,3,2,1,0:T(8,128)(2,1)S(1)} %shard_map.68), channel_id=1, replica_groups={{0,2,4,6},{1,3,5,7},{8,10,12,14},{9,11,13,15},{16,18,20,22},{17,19,21,2..., dimensions={0} | all-to-all | bytes 1048576 | tf_op jit(solution)/shard_map/all_to_all | solution.py:383
  49.5 0.0 collective-permute-start.3
  49.5 1.9 %collective-permute-done.3.other_ref = bf16[4,2,2,128,128]{4,3,2,1,0:T(8,128)(2,1)S(1)} collective-permute-done((bf16[4,2,2,128,128]{4,3,2,1,0:T(8,128)(2,1)S(1)}, bf16[4,2,2,128,128]{4,3,2,1,0:T(8,128)(2,1)S(1)}, u32[]{:S(2)}, u32[]{:S(2)}) %collective-permute-start.3) | collective-permute-done | bytes 524320 | tf_op jit(solution)/shard_map/ppermute | solution.py:160
  51.4 0.0 copy-done.2
  51.4 1.5 %shard_map.69 = bf16[5,2,128,128]{3,2,1,0:T(8,128)(2,1)} custom-call(s32[2,18]{1,0:T(2,128)S(1)} %copy-done, s32[1,2,4]{2,1,0:T(2,128)S(1)} %copy-done.2, bf16[4,2,2,128,128]{4,3,2,1,0:T(8,128)(2,1)S(1)} %all_to_all.10.same_ref, bf16[4,2,2,128,128]{4,3,2,1,0:T(8,128)(2,1)S(1)} %collective-permute-done.3.other_ref), custom_call_target="tpu_custom_call" | custom-call | bytes 1000000 | tf_op jit(solution)/shard_map/pallas_call | solution.py:344
  (1 shorter events, 0.0 us)
Async XLA Ops:
  4.8 5.3 %copy-start.3 = (bf16[2,5,2,128,128]{4,3,2,1,0:T(8,128)(2,1)S(1)}, bf16[2,5,2,128,128]{4,3,2,1,0:T(8,128)(2,1)}, u32[]{:S(2)}) copy-start(bf16[2,5,2,128,128]{4,3,2,1,0:T(8,128)(2,1)} %get-tuple-element.12) | copy-start | bytes 1966084
  4.8 22.6 %all-to-all-start = ((bf16[8,2,2,128,128]{4,3,2,1,0:T(8,128)(2,1)}), bf16[8,2,2,128,128]{4,3,2,1,0:T(8,128)(2,1)S(1)}, u32[]{:S(2)}, u32[]{:S(2)}) async-start(bf16[8,2,2,128,128]{4,3,2,1,0:T(8,128)(2,1)} %get-tuple-element.11), calls=%async_computation | async-start | bytes 2097152 | tf_op jit(solution)/shard_map/all_to_all | solution.py:371
  10.1 2.4 %copy-start = (s32[2,18]{1,0:T(2,128)S(1)}, s32[2,18]{1,0:T(2,128)}, u32[]{:S(2)}) copy-start(s32[2,18]{1,0:T(2,128)} %get-tuple-element.9.order_ref) | copy-start | bytes 436
  10.1 2.3 %collective-permute-start = (bf16[2,5,2,128,128]{4,3,2,1,0:T(8,128)(2,1)S(1)}, bf16[2,5,2,128,128]{4,3,2,1,0:T(8,128)(2,1)S(1)}, u32[]{:S(2)}, u32[]{:S(2)}) collective-permute-start(bf16[2,5,2,128,128]{4,3,2,1,0:T(8,128)(2,1)S(1)} %copy-done.3), channel_id=1, source_target_pairs={{0,1},{1,0},{2,3},{3,2},{4,5},{5,4},{6,7},{7,6},{8,9},{9,8},{10,11... | collective-permute-start | bytes 1966088 | tf_op jit(solution)/shard_map/ppermute | solution.py:160
  10.7 16.6 %copy-start.1 = (s32[2,18]{1,0:T(2,128)S(1)}, s32[2,18]{1,0:T(2,128)}, u32[]{:S(2)}) copy-start(s32[2,18]{1,0:T(2,128)} %get-tuple-element.10.flags_ref) | copy-start | bytes 436
  13.1 14.2 %collective-permute-start.1 = (bf16[2,2,128,128]{3,2,1,0:T(8,128)(2,1)S(1)}, bf16[2,2,128,128]{3,2,1,0:T(8,128)(2,1)S(1)}, u32[]{:S(2)}, u32[]{:S(2)}) collective-permute-start(bf16[2,2,128,128]{3,2,1,0:T(8,128)(2,1)S(1)} %shard_map.65), channel_id=1, source_target_pairs={{0,2},{1,3},{2,0},{3,1},{4,6},{5,7},{6,4},{7,5},{8,10},{9,11},{10,... | collective-permute-start | bytes 393224 | tf_op jit(solution)/shard_map/ppermute | solution.py:160
  29.4 8.8 %collective-permute-start.2 = (bf16[2,2,128,128]{3,2,1,0:T(8,128)(2,1)S(1)}, bf16[2,2,128,128]{3,2,1,0:T(8,128)(2,1)S(1)}, u32[]{:S(2)}, u32[]{:S(2)}) collective-permute-start(bf16[2,2,128,128]{3,2,1,0:T(8,128)(2,1)S(1)} %shard_map.67), channel_id=1, source_target_pairs={{0,16},{8,24},{16,0},{24,8},{1,17},{9,25},{17,1},{25,9},{2,18},{10... | collective-permute-start | bytes 393224 | tf_op jit(solution)/shard_map/ppermute | solution.py:378
  35.0 16.3 %copy-start.2 = (s32[1,2,4]{2,1,0:T(2,128)S(1)}, s32[1,2,4]{2,1,0:T(2,128)}, u32[]{:S(2)}) copy-start(s32[1,2,4]{2,1,0:T(2,128)} %counts_ref.3) | copy-start | bytes 100
  49.5 1.9 %collective-permute-start.3 = (bf16[4,2,2,128,128]{4,3,2,1,0:T(8,128)(2,1)S(1)}, bf16[4,2,2,128,128]{4,3,2,1,0:T(8,128)(2,1)S(1)}, u32[]{:S(2)}, u32[]{:S(2)}) collective-permute-start(bf16[4,2,2,128,128]{4,3,2,1,0:T(8,128)(2,1)S(1)} %all_to_all.10.same_ref), channel_id=1, source_target_pairs={{0,1},{1,0},{2,3},{3,2},{4,5},{5,4},{6,7},{7,6},{8,9},{9,8},{10,11... | collective-permute-start | bytes 1572872 | tf_op jit(solution)/shard_map/ppermute | solution.py:160

commit v2 on v1

--- a/solution.py
+++ b/solution.py
@@ -98,61 +98,82 @@
         filled[1] = filled[1] + count(really & jnp.logical_not(room))
 
 
-def pack_kernel(
-    per_half, rows_ref, cols_ref, counts_ref, down_ref, up_ref, w_ref,
+def pick(which, per_half, owners, rows_ref, order_ref, x_ref, out_ref, sems):
+    copies, used = [], [unit_place(unit, per_half, owners) for unit in range(2 * per_half)]
+    for i in range(4 * per_half):
+        row = rows_ref[0, which, jnp.maximum(order_ref[which, i], 0)]
+        at = pl.multiple_of(row * TILE, TILE)
+        copy = pltpu.make_async_copy(
+            x_ref.at[0, 0, :, pl.ds(at, TILE)], out_ref.at[used[i // 2], i % 2], sems.at[i]
+        )
+        copy.start()
+        copies.append(copy)
+    for place in range(out_ref.shape[0]):
+        if place not in used:
+            out_ref[place] = jnp.zeros(out_ref.shape[1:], out_ref.dtype)
+    return copies
+
+
+def pack_up_kernel(
+    per_half, rows_ref, cols_ref, counts_ref, x_ref, w_ref,
     out_ref, own_w_ref, order_ref, flags_ref, first_ref, last_ref, sems, w_sem,
 ):
     slots, owners = cols_ref.shape[2], counts_ref.shape[2]
-    places, units = out_ref.shape[0], 2 * per_half
-    copies = [pltpu.make_async_copy(w_ref.at[0], own_w_ref, w_sem)]
-    copies[0].start()
-    used = [unit_place(unit, per_half, owners) for unit in range(units)]
-    for which, x_ref in ((1, up_ref), (0, down_ref)):
-        order_units(
-            cols_ref, counts_ref, which, slots, per_half, order_ref, flags_ref, first_ref, last_ref
-        )
-        for i in range(2 * units):
-            row = rows_ref[0, which, jnp.maximum(order_ref[which, i], 0)]
-            at = pl.multiple_of(row * TILE, TILE)
-            copy = pltpu.make_async_copy(
-                x_ref.at[0, 0, :, pl.ds(at, TILE)],
-                out_ref.at[used[i // 2], which, i % 2],
-                sems.at[which, i],
-            )
-            copy.start()
-            copies.append(copy)
-    for place in range(places):
-        if place not in used:
-            out_ref[place] = jnp.zeros(out_ref.shape[1:], out_ref.dtype)
-    for copy in copies:
+    weights = pltpu.make_async_copy(w_ref.at[0], own_w_ref, w_sem)
+    weights.start()
+    tables = (order_ref, flags_ref, first_ref, last_ref)
+    order_units(cols_ref, counts_ref, 1, slots, per_half, *tables)
+    copies = pick(1, per_half, owners, rows_ref, order_ref, x_ref, out_ref, sems)
+    order_units(cols_ref, counts_ref, 0, slots, per_half, *tables)
+    for copy in copies + [weights]:
         copy.wait()
 
 
-def pack(x_down, x_up, w_tiles, tile_rows, tile_cols, counts, per_half, places):
-    rows, units = x_down.shape[2], 2 * per_half
+def pack_up(x_up, w_tiles, tile_rows, tile_cols, counts, per_half, places):
+    rows, units = x_up.shape[2], 2 * per_half
     smem = pl.BlockSpec(memory_space=pltpu.SMEM)
     vmem = pl.BlockSpec(memory_space=pltpu.VMEM)
     hbm = pl.BlockSpec(memory_space=pl.ANY)
     return pl.pallas_call(
-        functools.partial(pack_kernel, per_half),
+        functools.partial(pack_up_kernel, per_half),
         out_shape=[
-            jax.ShapeDtypeStruct((places, 2, 2, rows, TILE), x_down.dtype),
+            jax.ShapeDtypeStruct((places, 2, rows, TILE), x_up.dtype),
             jax.ShapeDtypeStruct(w_tiles.shape[1:], w_tiles.dtype),
             jax.ShapeDtypeStruct((2, 2 * units + 2), jnp.int32),
             jax.ShapeDtypeStruct((2, 2 * units + 2), jnp.int32),
         ],
-        in_specs=[smem, smem, smem, hbm, hbm, hbm],
+        in_specs=[smem, smem, smem, hbm, hbm],
         out_specs=[vmem, vmem, smem, smem],
         scratch_shapes=[
             pltpu.SMEM((COLUMNS + 1,), jnp.int32),
             pltpu.SMEM((COLUMNS + 1,), jnp.int32),
-            pltpu.SemaphoreType.DMA((2, 2 * units)),
+            pltpu.SemaphoreType.DMA((2 * units,)),
             pltpu.SemaphoreType.DMA,
         ],
         cost_estimate=pl.CostEstimate(
-            flops=0, bytes_accessed=16 * units * rows * TILE, transcendentals=0
+            flops=0, bytes_accessed=8 * units * rows * TILE, transcendentals=0
         ),
-    )(tile_rows, tile_cols, counts, x_down, x_up, w_tiles)
+    )(tile_rows, tile_cols, counts, x_up, w_tiles)
+
+
+def pack_down_kernel(per_half, owners, rows_ref, order_ref, x_ref, out_ref, sems):
+    for copy in pick(0, per_half, owners, rows_ref, order_ref, x_ref, out_ref, sems):
+        copy.wait()
+
+
+def pack_down(x_down, tile_rows, order, per_half, owners, places):
+    rows, units = x_down.shape[2], 2 * per_half
+    smem = pl.BlockSpec(memory_space=pltpu.SMEM)
+    return pl.pallas_call(
+        functools.partial(pack_down_kernel, per_half, owners),
+        out_shape=jax.ShapeDtypeStruct((places, 2, rows, TILE), x_down.dtype),
+        in_specs=[smem, smem, pl.BlockSpec(memory_space=pl.ANY)],
+        out_specs=pl.BlockSpec(memory_space=pltpu.VMEM),
+        scratch_shapes=[pltpu.SemaphoreType.DMA((2 * units,))],
+        cost_estimate=pl.CostEstimate(
+            flops=0, bytes_accessed=8 * units * rows * TILE, transcendentals=0
+        ),
+    )(tile_rows, order, x_down)
 
 
 def swapped(array, apart):
@@ -197,7 +218,7 @@
     which, per_half, owners, loss_scale, order_ref, flags_ref, x_ref, near_ref, far_ref, out_ref,
     w_unit, first_sum, second_sum,
 ):
-    sources, _, _, rows, _ = x_ref.shape
+    sources, _, rows, _ = x_ref.shape
     per_owner = near_ref.shape[1] // CORES
     unit = unit_here(per_half, owners)
     half = lax.axis_index("fsdp") // CORES
@@ -222,7 +243,7 @@
     def read(step):
         at = step * together
         return [
-            x_ref[pl.ds(at, together), which, i].reshape(together * rows, TILE) for i in range(2)
+            x_ref[pl.ds(at, together), i].reshape(together * rows, TILE) for i in range(2)
         ]
 
     @pl.when(coupled)
@@ -267,7 +288,7 @@
 
 
 def unit_grads(which, blocks, near, far, order, flags, per_half, owners, loss_scale, dtype):
-    sources, _, _, rows, _ = blocks.shape
+    sources, _, rows, _ = blocks.shape
     smem = pl.BlockSpec(memory_space=pltpu.SMEM)
     vmem = pl.BlockSpec(memory_space=pltpu.VMEM)
     return pl.pallas_call(
@@ -365,18 +386,20 @@
     across = [(i, (i + sections // 2) % sections) for i in range(sections)]
     loss_scale = float(2 * rows_here * places) ** (-0.5)
 
-    packed, own_w, order, flags = pack(
-        x_down, x_up, w_tiles, tile_rows, tile_cols, counts, per_half, places
-    )
-    blocks = lax.all_to_all(packed, PLANE, split_axis=0, concat_axis=0, tiled=True)
+    trade = lambda packed: lax.all_to_all(packed, PLANE, split_axis=0, concat_axis=0, tiled=True)
+    up, own_w, order, flags = pack_up(
+        x_up, w_tiles, tile_rows, tile_cols, counts, per_half, places
+    )
+    up = trade(up)
+    down = trade(pack_down(x_down, tile_rows, order, per_half, owners, places))
     near = jnp.concatenate([own_w, swapped(own_w, 1)], axis=1)
     far = swapped(far_weights(near, order, per_half), CORES)
     grads = functools.partial(
-        unit_grads, blocks=blocks, near=near, far=far, order=order, flags=flags,
+        unit_grads, near=near, far=far, order=order, flags=flags,
         per_half=per_half, owners=owners, loss_scale=loss_scale,
     )
-    arrived = lax.ppermute(grads(1, dtype=jnp.bfloat16), "section", across)
-    mine = add(grads(0, dtype=jnp.float32), arrived, places // CORES)
+    arrived = lax.ppermute(grads(1, up, dtype=jnp.bfloat16), "section", across)
+    mine = add(grads(0, down, dtype=jnp.float32), arrived, places // CORES)
     same_core = [
         [place for place in range(places) if place % CORES == core] for core in range(CORES)
     ]

time: 53.1 us -> 59.5 us (1.12)
  starting transfers between devices: 10.9 us -> 13.5 us
  Pallas kernels: 11.5 us -> 13.3 us
  local copies, waits for them, and re-layouts: 0.17 us -> 1.26 us
  waiting for transfers between devices: 19.1 us -> 19.7 us
    ppermute x3, waiting for transfers between devices: 15.9 us -> 9.58 us  [swapped(): return lax.ppermute(array, 'fsdp', [(i, i ^ apart) for i in range(size)])]
    all_to_all x1 -> x2, waiting for transfers between devices: 0.01 us -> 6.04 us  [body(): lax.all_to_all(packed, PLANE, split_axis=0, concat_axis=0, tiled=True)]
    all_to_all x1 -> x2, starting transfers between devices: 5.31 us -> 8.32 us  [body(): lax.all_to_all(packed, PLANE, split_axis=0, concat_axis=0, tiled=True)]
    pallas_call x1 -> x2, Pallas kernels: 4.76 us -> 7.07 us  [the longest x1 4.28 us: pack_up(): pl.pallas_call(functools.partial(pack_up_kernel, per_half), out_shape=[ja...]
    concatenate x1, local copies, waits for them, and re-layouts: 0.1 us -> 1.19 us  [body(): near = jnp.concatenate([own_w, swapped(own_w, 1)], axis=1)]
    ppermute x1, waiting for transfers between devices: 3.2 us -> 4.07 us  [body(): arrived = lax.ppermute(grads(1, up, dtype=jnp.bfloat16), 'section', across)]
  transfers between devices with their start and end apart: 5 -> 6, of which waited for: 4 -> 4; matrix products, arithmetic and copies ran while one was open for 0% -> 2% of each run, Pallas kernels for 6% -> 13%
where the time goes in v2:
time: 59.5 us; the launch traced here: 59 us
  waiting for transfers between devices  19.7 us (33%)
  starting transfers between devices  13.5 us (23%)
  Pallas kernels  13.3 us (22%)
  blocking collectives  11.2 us (19%)
  local copies, waits for them, and re-layouts  1.26 us (2%)
    all_to_all x1, blocking collectives, body(): lax.all_to_all(mine, PLANE, split_axis=0, concat_axis=0, axis_index_group...  11.2 us
    ppermute x3, waiting for transfers between devices, swapped(): return lax.ppermute(array, 'fsdp', [(i, i ^ apart) for i in range(size)])  9.58 us
    all_to_all x2, starting transfers between devices, body(): lax.all_to_all(packed, PLANE, split_axis=0, concat_axis=0, tiled=True)  8.32 us
    all_to_all x2, waiting for transfers between devices, body(): lax.all_to_all(packed, PLANE, split_axis=0, concat_axis=0, tiled=True)  6.04 us
    pallas_call x1, Pallas kernels, pack_up(): pl.pallas_call(functools.partial(pack_up_kernel, per_half), out_shape=[ja...  4.28 us
    pallas_call x2, Pallas kernels, unit_grads(): pl.pallas_call(functools.partial(grads_kernel, which, per_half, owners, l...  4.13 us
    ppermute x1, waiting for transfers between devices, body(): arrived = lax.ppermute(grads(1, up, dtype=jnp.bfloat16), 'section', across)  4.07 us
    pallas_call x1, Pallas kernels, pack_down(): pl.pallas_call(functools.partial(pack_down_kernel, per_half, owners), out...  2.79 us
  transfers between devices with their start and end apart: 6, of which 4 were waited for; matrix products, arithmetic and copies ran while one was open for 2% of the time, Pallas kernels for 13%

profile of v2, /device:TPU:0, one launch (start us, length us, event | category | flops | bytes accessed | tf_op | source)
XLA Modules:
  0.0 59.0 jit_solution(17624818767104118001)
XLA Ops:
  0.0 4.3 %shard_map.64 = (bf16[8,2,128,128]{3,2,1,0:T(8,128)(2,1)}, bf16[2,5,2,128,128]{4,3,2,1,0:T(8,128)(2,1)}, s32[2,18]{1,0:T(2,128)}, s32[2,18]{1,0:T(2,128)}) custom-call(s32[1,2,20]{2,1,0:T(2,128)} %rows_ref.3, s32[1,2,20]{2,1,0:T(2,128)} %cols_ref.1, s32[1,2,4]{2,1,0:T(2,128)} %counts_ref.3, bf16[1,1,128,6144]{3,2,1,0:T(8,128)(2,1)} %x_ref.2, ...), custom_call_target="tpu_custom_call" | custom-call | bytes 1048576 | tf_op jit(solution)/shard_map/pallas_call | solution.py:137
  4.3 0.5 collective-permute-start
  4.8 4.8 %all-to-all-start.1 = ((bf16[8,2,128,128]{3,2,1,0:T(8,128)(2,1)}), bf16[8,2,128,128]{3,2,1,0:T(8,128)(2,1)S(1)}, u32[]{:S(2)}, u32[]{:S(2)}) async-start(bf16[8,2,128,128]{3,2,1,0:T(8,128)(2,1)} %get-tuple-element.12), calls=%async_computation.1 | async-start | bytes 1048576 | tf_op jit(solution)/shard_map/all_to_all | solution.py:389
  9.6 0.0 copy-start.3
  9.6 2.8 %shard_map.65 = bf16[8,2,128,128]{3,2,1,0:T(8,128)(2,1)} custom-call(s32[1,2,20]{2,1,0:T(2,128)} %rows_ref.3, s32[2,18]{1,0:T(2,128)} %get-tuple-element.9.order_ref, bf16[1,1,128,6144]{3,2,1,0:T(8,128)(2,1)} %x_ref.3), custom_call_target="tpu_custom_call" | custom-call | bytes 1048576 | tf_op jit(solution)/shard_map/pallas_call | solution.py:167
  12.4 6.0 %all-to-all-done.1.x_ref = bf16[8,2,128,128]{3,2,1,0:T(8,128)(2,1)S(1)} async-done(((bf16[8,2,128,128]{3,2,1,0:T(8,128)(2,1)}), bf16[8,2,128,128]{3,2,1,0:T(8,128)(2,1)S(1)}, u32[]{:S(2)}, u32[]{:S(2)}) %all-to-all-start.1) | async-done | bytes 524320 | tf_op jit(solution)/shard_map/all_to_all | solution.py:389
  18.5 3.5 %all-to-all-start = ((bf16[8,2,128,128]{3,2,1,0:T(8,128)(2,1)}), bf16[8,2,128,128]{3,2,1,0:T(8,128)(2,1)S(1)}, u32[]{:S(2)}, u32[]{:S(2)}) async-start(bf16[8,2,128,128]{3,2,1,0:T(8,128)(2,1)} %shard_map.65), calls=%async_computation | async-start | bytes 1048576 | tf_op jit(solution)/shard_map/all_to_all | solution.py:389
  22.0 0.0 copy-done.3
  22.0 0.0 copy-start
  22.0 0.1 constant_dynamic-update-slice_fusion.1
  22.1 0.0 copy-start.1
  22.1 0.0 collective-permute-done
  22.1 1.2 %constant_dynamic-update-slice_fusion.near_ref = bf16[2,10,2,128,128]{4,3,2,1,0:T(8,128)(2,1)S(1)} fusion(bf16[2,10,2,128,128]{4,3,2,1,0:T(8,128)(2,1)S(1)} %constant_dynamic-update-slice_fusion.1, bf16[2,5,2,128,128]{4,3,2,1,0:T(8,128)(2,1)} %collective-permute-done), kind=kLoop, calls=%fused_computation | loop fusion | bytes 1310720 | tf_op jit(solution)/shard_map/concatenate | solution.py:395
  23.3 0.0 copy-done
  23.3 0.6 %shard_map.66 = bf16[2,2,128,128]{3,2,1,0:T(8,128)(2,1)S(1)} custom-call(s32[2,18]{1,0:T(2,128)S(1)} %copy-done, bf16[2,10,2,128,128]{4,3,2,1,0:T(8,128)(2,1)S(1)} %constant_dynamic-update-slice_fusion.near_ref), custom_call_target="tpu_custom_call" | custom-call | bytes 300000 | tf_op jit(solution)/shard_map/pallas_call | solution.py:201
  23.9 2.0 %collective-permute-start.1 = (bf16[2,2,128,128]{3,2,1,0:T(8,128)(2,1)S(1)}, bf16[2,2,128,128]{3,2,1,0:T(8,128)(2,1)S(1)}, u32[]{:S(2)}, u32[]{:S(2)}) collective-permute-start(bf16[2,2,128,128]{3,2,1,0:T(8,128)(2,1)S(1)} %shard_map.66), channel_id=1, source_target_pairs={{0,2},{1,3},{2,0},{3,1},{4,6},{5,7},{6,4},{7,5},{8,10},{9,11},{10,... | collective-permute-start | bytes 393224 | tf_op jit(solution)/shard_map/ppermute | solution.py:181
  25.9 7.7 %collective-permute-done.1.far_ref = bf16[2,2,128,128]{3,2,1,0:T(8,128)(2,1)S(1)} collective-permute-done((bf16[2,2,128,128]{3,2,1,0:T(8,128)(2,1)S(1)}, bf16[2,2,128,128]{3,2,1,0:T(8,128)(2,1)S(1)}, u32[]{:S(2)}, u32[]{:S(2)}) %collective-permute-start.1) | collective-permute-done | bytes 131104 | tf_op jit(solution)/shard_map/ppermute | solution.py:181
  33.5 0.0 copy-done.1
  33.6 2.1 %shard_map.68 = bf16[2,2,128,128]{3,2,1,0:T(8,128)(2,1)S(1)} custom-call(s32[2,18]{1,0:T(2,128)S(1)} %copy-done, s32[2,18]{1,0:T(2,128)S(1)} %copy-done.1, bf16[8,2,128,128]{3,2,1,0:T(8,128)(2,1)S(1)} %all-to-all-done.1.x_ref, bf16[2,10,2,128,128]{4,3,2,1,0:T(8,128)(2,1)S(1)} %constant_dynamic-update-slice_fusion.near_ref, ...), custom_call_target="tpu_custom_call" | custom-call | flops 335544320 | bytes 524288 | tf_op jit(solution)/shard_map/pallas_call | solution.py:294
  35.6 2.7 %collective-permute-start.2 = (bf16[2,2,128,128]{3,2,1,0:T(8,128)(2,1)S(1)}, bf16[2,2,128,128]{3,2,1,0:T(8,128)(2,1)S(1)}, u32[]{:S(2)}, u32[]{:S(2)}) collective-permute-start(bf16[2,2,128,128]{3,2,1,0:T(8,128)(2,1)S(1)} %shard_map.68), channel_id=1, source_target_pairs={{0,16},{8,24},{16,0},{24,8},{1,17},{9,25},{17,1},{25,9},{2,18},{10... | collective-permute-start | bytes 393224 | tf_op jit(solution)/shard_map/ppermute | solution.py:401
  38.3 0.0 all-to-all-done.x_ref
  38.3 2.1 %shard_map.67.own_ref = f32[2,2,128,128]{3,2,1,0:T(8,128)S(1)} custom-call(s32[2,18]{1,0:T(2,128)S(1)} %copy-done, s32[2,18]{1,0:T(2,128)S(1)} %copy-done.1, bf16[8,2,128,128]{3,2,1,0:T(8,128)(2,1)S(1)} %all-to-all-done.x_ref, bf16[2,10,2,128,128]{4,3,2,1,0:T(8,128)(2,1)S(1)} %constant_dynamic-update-slice_fusion.near_ref, ...), custom_call_target="tpu_custom_call" | custom-call | flops 335544320 | bytes 524288 | tf_op jit(solution)/shard_map/pallas_call | solution.py:294
  40.4 0.0 copy-start.2
  40.4 4.1 %collective-permute-done.2.arrived_ref = bf16[2,2,128,128]{3,2,1,0:T(8,128)(2,1)S(1)} collective-permute-done((bf16[2,2,128,128]{3,2,1,0:T(8,128)(2,1)S(1)}, bf16[2,2,128,128]{3,2,1,0:T(8,128)(2,1)S(1)}, u32[]{:S(2)}, u32[]{:S(2)}) %collective-permute-start.2) | collective-permute-done | bytes 131104 | tf_op jit(solution)/shard_map/ppermute | solution.py:401
  44.5 11.2 %all_to_all.15.same_ref = bf16[4,2,2,128,128]{4,3,2,1,0:T(8,128)(2,1)S(1)} all-to-all(bf16[4,2,2,128,128]{4,3,2,1,0:T(8,128)(2,1)S(1)} %shard_map.69), channel_id=1, replica_groups={{0,2,4,6},{1,3,5,7},{8,10,12,14},{9,11,13,15},{16,18,20,22},{17,19,21,2..., dimensions={0} | all-to-all | bytes 1048576 | tf_op jit(solution)/shard_map/all_to_all | solution.py:406
  55.7 0.0 collective-permute-start.3
  55.7 1.9 %collective-permute-done.3.other_ref = bf16[4,2,2,128,128]{4,3,2,1,0:T(8,128)(2,1)S(1)} collective-permute-done((bf16[4,2,2,128,128]{4,3,2,1,0:T(8,128)(2,1)S(1)}, bf16[4,2,2,128,128]{4,3,2,1,0:T(8,128)(2,1)S(1)}, u32[]{:S(2)}, u32[]{:S(2)}) %collective-permute-start.3) | collective-permute-done | bytes 524320 | tf_op jit(solution)/shard_map/ppermute | solution.py:181
  57.6 0.0 copy-done.2
  57.6 1.5 %shard_map.70 = bf16[5,2,128,128]{3,2,1,0:T(8,128)(2,1)} custom-call(s32[2,18]{1,0:T(2,128)S(1)} %copy-done, s32[1,2,4]{2,1,0:T(2,128)S(1)} %copy-done.2, bf16[4,2,2,128,128]{4,3,2,1,0:T(8,128)(2,1)S(1)} %all_to_all.15.same_ref, bf16[4,2,2,128,128]{4,3,2,1,0:T(8,128)(2,1)S(1)} %collective-permute-done.3.other_ref), custom_call_target="tpu_custom_call" | custom-call | bytes 1000000 | tf_op jit(solution)/shard_map/pallas_call | solution.py:365
  (1 shorter events, 0.0 us)
Async XLA Ops:
  4.3 17.8 %collective-permute-start = (bf16[2,5,2,128,128]{4,3,2,1,0:T(8,128)(2,1)}, bf16[2,5,2,128,128]{4,3,2,1,0:T(8,128)(2,1)}, u32[]{:S(2)}, u32[]{:S(2)}) collective-permute-start(bf16[2,5,2,128,128]{4,3,2,1,0:T(8,128)(2,1)} %get-tuple-element.11), channel_id=1, source_target_pairs={{0,1},{1,0},{2,3},{3,2},{4,5},{5,4},{6,7},{7,6},{8,9},{9,8},{10,11... | collective-permute-start | bytes 1966088 | tf_op jit(solution)/shard_map/ppermute | solution.py:181
  4.8 13.7 %all-to-all-start.1 = ((bf16[8,2,128,128]{3,2,1,0:T(8,128)(2,1)}), bf16[8,2,128,128]{3,2,1,0:T(8,128)(2,1)S(1)}, u32[]{:S(2)}, u32[]{:S(2)}) async-start(bf16[8,2,128,128]{3,2,1,0:T(8,128)(2,1)} %get-tuple-element.12), calls=%async_computation.1 | async-start | bytes 1048576 | tf_op jit(solution)/shard_map/all_to_all | solution.py:389
  9.6 12.3 %copy-start.3 = (bf16[2,5,2,128,128]{4,3,2,1,0:T(8,128)(2,1)S(1)}, bf16[2,5,2,128,128]{4,3,2,1,0:T(8,128)(2,1)}, u32[]{:S(2)}) copy-start(bf16[2,5,2,128,128]{4,3,2,1,0:T(8,128)(2,1)} %get-tuple-element.11) | copy-start | bytes 1966084
  18.5 19.8 %all-to-all-start = ((bf16[8,2,128,128]{3,2,1,0:T(8,128)(2,1)}), bf16[8,2,128,128]{3,2,1,0:T(8,128)(2,1)S(1)}, u32[]{:S(2)}, u32[]{:S(2)}) async-start(bf16[8,2,128,128]{3,2,1,0:T(8,128)(2,1)} %shard_map.65), calls=%async_computation | async-start | bytes 1048576 | tf_op jit(solution)/shard_map/all_to_all | solution.py:389
  22.0 1.3 %copy-start = (s32[2,18]{1,0:T(2,128)S(1)}, s32[2,18]{1,0:T(2,128)}, u32[]{:S(2)}) copy-start(s32[2,18]{1,0:T(2,128)} %get-tuple-element.9.order_ref) | copy-start | bytes 436
  22.1 11.5 %copy-start.1 = (s32[2,18]{1,0:T(2,128)S(1)}, s32[2,18]{1,0:T(2,128)}, u32[]{:S(2)}) copy-start(s32[2,18]{1,0:T(2,128)} %get-tuple-element.10.flags_ref) | copy-start | bytes 436
  23.9 9.6 %collective-permute-start.1 = (bf16[2,2,128,128]{3,2,1,0:T(8,128)(2,1)S(1)}, bf16[2,2,128,128]{3,2,1,0:T(8,128)(2,1)S(1)}, u32[]{:S(2)}, u32[]{:S(2)}) collective-permute-start(bf16[2,2,128,128]{3,2,1,0:T(8,128)(2,1)S(1)} %shard_map.66), channel_id=1, source_target_pairs={{0,2},{1,3},{2,0},{3,1},{4,6},{5,7},{6,4},{7,5},{8,10},{9,11},{10,... | collective-permute-start | bytes 393224 | tf_op jit(solution)/shard_map/ppermute | solution.py:181
  35.6 8.8 %collective-permute-start.2 = (bf16[2,2,128,128]{3,2,1,0:T(8,128)(2,1)S(1)}, bf16[2,2,128,128]{3,2,1,0:T(8,128)(2,1)S(1)}, u32[]{:S(2)}, u32[]{:S(2)}) collective-permute-start(bf16[2,2,128,128]{3,2,1,0:T(8,128)(2,1)S(1)} %shard_map.68), channel_id=1, source_target_pairs={{0,16},{8,24},{16,0},{24,8},{1,17},{9,25},{17,1},{25,9},{2,18},{10... | collective-permute-start | bytes 393224 | tf_op jit(solution)/shard_map/ppermute | solution.py:401
  40.4 17.2 %copy-start.2 = (s32[1,2,4]{2,1,0:T(2,128)S(1)}, s32[1,2,4]{2,1,0:T(2,128)}, u32[]{:S(2)}) copy-start(s32[1,2,4]{2,1,0:T(2,128)} %counts_ref.3) | copy-start | bytes 100
  55.7 1.9 %collective-permute-start.3 = (bf16[4,2,2,128,128]{4,3,2,1,0:T(8,128)(2,1)S(1)}, bf16[4,2,2,128,128]{4,3,2,1,0:T(8,128)(2,1)S(1)}, u32[]{:S(2)}, u32[]{:S(2)}) collective-permute-start(bf16[4,2,2,128,128]{4,3,2,1,0:T(8,128)(2,1)S(1)} %all_to_all.15.same_ref), channel_id=1, source_target_pairs={{0,1},{1,0},{2,3},{3,2},{4,5},{5,4},{6,7},{7,6},{8,9},{9,8},{10,11... | collective-permute-start | bytes 1572872 | tf_op jit(solution)/shard_map/ppermute | solution.py:181

commit v3 on v1

--- a/solution.py
+++ b/solution.py
@@ -10,7 +10,7 @@
 
 TILE = 128
 PLANE = ("dp", "fsdp")
-SOURCES_AT_ONCE = 4
+SOURCES_AT_ONCE = 8
 COLUMNS = 192
 CORES = 2
 IN_VMEM = pltpu.CompilerParams(vmem_limit_bytes=16 * 1024 * 1024)
@@ -99,13 +99,12 @@
 
 
 def pack_kernel(
-    per_half, rows_ref, cols_ref, counts_ref, down_ref, up_ref, w_ref,
-    out_ref, own_w_ref, order_ref, flags_ref, first_ref, last_ref, sems, w_sem,
+    per_half, rows_ref, cols_ref, counts_ref, down_ref, up_ref,
+    out_ref, order_ref, flags_ref, first_ref, last_ref, sems,
 ):
     slots, owners = cols_ref.shape[2], counts_ref.shape[2]
     places, units = out_ref.shape[0], 2 * per_half
-    copies = [pltpu.make_async_copy(w_ref.at[0], own_w_ref, w_sem)]
-    copies[0].start()
+    copies = []
     used = [unit_place(unit, per_half, owners) for unit in range(units)]
     for which, x_ref in ((1, up_ref), (0, down_ref)):
         order_units(
@@ -128,7 +127,7 @@
         copy.wait()
 
 
-def pack(x_down, x_up, w_tiles, tile_rows, tile_cols, counts, per_half, places):
+def pack(x_down, x_up, tile_rows, tile_cols, counts, per_half, places):
     rows, units = x_down.shape[2], 2 * per_half
     smem = pl.BlockSpec(memory_space=pltpu.SMEM)
     vmem = pl.BlockSpec(memory_space=pltpu.VMEM)
@@ -137,22 +136,20 @@
         functools.partial(pack_kernel, per_half),
         out_shape=[
             jax.ShapeDtypeStruct((places, 2, 2, rows, TILE), x_down.dtype),
-            jax.ShapeDtypeStruct(w_tiles.shape[1:], w_tiles.dtype),
             jax.ShapeDtypeStruct((2, 2 * units + 2), jnp.int32),
             jax.ShapeDtypeStruct((2, 2 * units + 2), jnp.int32),
         ],
-        in_specs=[smem, smem, smem, hbm, hbm, hbm],
-        out_specs=[vmem, vmem, smem, smem],
+        in_specs=[smem, smem, smem, hbm, hbm],
+        out_specs=[vmem, smem, smem],
         scratch_shapes=[
             pltpu.SMEM((COLUMNS + 1,), jnp.int32),
             pltpu.SMEM((COLUMNS + 1,), jnp.int32),
             pltpu.SemaphoreType.DMA((2, 2 * units)),
-            pltpu.SemaphoreType.DMA,
         ],
         cost_estimate=pl.CostEstimate(
             flops=0, bytes_accessed=16 * units * rows * TILE, transcendentals=0
         ),
-    )(tile_rows, tile_cols, counts, x_down, x_up, w_tiles)
+    )(tile_rows, tile_cols, counts, x_down, x_up)
 
 
 def swapped(array, apart):
@@ -213,10 +210,15 @@
         def _():
             w_unit[i] = far_ref[which]
 
-    first_sum[...] = jnp.zeros_like(first_sum)
-    second_sum[...] = jnp.zeros_like(second_sum)
     together = min(SOURCES_AT_ONCE, sources)
     steps = sources // together
+    if steps > 1:
+        first_sum[...] = jnp.zeros_like(first_sum)
+        second_sum[...] = jnp.zeros_like(second_sum)
+
+    def sum_up(total_ref, where, term):
+        total_ref[where] = total_ref[where] + term if steps > 1 else term
+
     coupled = flags_ref[which, 2 * unit] == 1
 
     def read(step):
@@ -237,8 +239,8 @@
             cotangent = (loss_scale * (xs.astype(jnp.float32) + delta)).astype(jnp.bfloat16)
             grad_act = dot(cotangent, seconds, 1, 1)
             grad_pre = (grad_act * slope).astype(jnp.bfloat16)
-            first_sum[...] += dot(xs, grad_pre, 0, 0)
-            second_sum[...] += dot(active, cotangent, 0, 0)
+            sum_up(first_sum, ..., dot(xs, grad_pre, 0, 0))
+            sum_up(second_sum, ..., dot(active, cotangent, 0, 0))
             return carry
 
         lax.fori_loop(0, steps, go, 0, unroll=min(steps, 4))
@@ -254,8 +256,8 @@
                 cotangent = (loss_scale * (x.astype(jnp.float32) + delta)).astype(jnp.bfloat16)
                 grad_act = dot(cotangent, w_unit[i, 1], 1, 1)
                 grad_pre = (grad_act * slope).astype(jnp.bfloat16)
-                first_sum[across, :] += dot(x, grad_pre, 0, 0)
-                second_sum[:, across] += dot(active, cotangent, 0, 0)
+                sum_up(first_sum, (across, slice(None)), dot(x, grad_pre, 0, 0))
+                sum_up(second_sum, (slice(None), across), dot(active, cotangent, 0, 0))
             return carry
 
         lax.fori_loop(0, steps, go, 0, unroll=min(steps, 4))
@@ -365,11 +367,9 @@
     across = [(i, (i + sections // 2) % sections) for i in range(sections)]
     loss_scale = float(2 * rows_here * places) ** (-0.5)
 
-    packed, own_w, order, flags = pack(
-        x_down, x_up, w_tiles, tile_rows, tile_cols, counts, per_half, places
-    )
+    packed, order, flags = pack(x_down, x_up, tile_rows, tile_cols, counts, per_half, places)
     blocks = lax.all_to_all(packed, PLANE, split_axis=0, concat_axis=0, tiled=True)
-    near = jnp.concatenate([own_w, swapped(own_w, 1)], axis=1)
+    near = jnp.concatenate([w_tiles[0], swapped(w_tiles[0], 1)], axis=1)
     far = swapped(far_weights(near, order, per_half), CORES)
     grads = functools.partial(
         unit_grads, blocks=blocks, near=near, far=far, order=order, flags=flags,

time: 53.1 us -> 52 us (0.979)
  Pallas kernels: 11.5 us -> 9.62 us
  other arithmetic: 0 us -> 1.21 us
  waiting for transfers between devices: 19.1 us -> 20 us
  starting transfers between devices: 10.9 us -> 10.2 us
  blocking collectives: 11.2 us -> 10.5 us
    ppermute x1, waiting for transfers between devices: 3.2 us -> 4.71 us  [body(): arrived = lax.ppermute(grads(1, dtype=jnp.bfloat16), 'section', across)]
    concatenate x0 -> x1, other arithmetic: none -> 1.21 us  [body(): near = jnp.concatenate([w_tiles[0], swapped(w_tiles[0], 1)], axis=1)]
    pallas_call x2, Pallas kernels: 4.57 us -> 3.38 us  [unit_grads(): pl.pallas_call(functools.partial(grads_kernel, which, per_half, owners, l...]
    all_to_all x1, blocking collectives: 11.2 us -> 10.5 us  [body(): lax.all_to_all(mine, PLANE, split_axis=0, concat_axis=0, axis_index_group...]
    pallas_call x1, Pallas kernels: 4.76 us -> 4.12 us  [pack(): pl.pallas_call(functools.partial(pack_kernel, per_half), out_shape=[jax.S...]
    ppermute x3, waiting for transfers between devices: 15.9 us -> 15.2 us  [swapped(): return lax.ppermute(array, 'fsdp', [(i, i ^ apart) for i in range(size)])]
  transfers between devices with their start and end apart: 5 -> 5, of which waited for: 4 -> 3; matrix products, arithmetic and copies ran while one was open for 0% -> 2% of each run, Pallas kernels for 6% -> 12%
where the time goes in v3:
time: 52 us; the launch traced here: 51.6 us
  waiting for transfers between devices  20 us (38%)
  blocking collectives  10.5 us (20%)
  starting transfers between devices  10.2 us (20%)
  Pallas kernels  9.62 us (18%)
  other arithmetic  1.21 us (2%)
    ppermute x3, waiting for transfers between devices, swapped(): return lax.ppermute(array, 'fsdp', [(i, i ^ apart) for i in range(size)])  15.2 us
    all_to_all x1, blocking collectives, body(): lax.all_to_all(mine, PLANE, split_axis=0, concat_axis=0, axis_index_group...  10.5 us
    all_to_all x1, starting transfers between devices, body(): lax.all_to_all(packed, PLANE, split_axis=0, concat_axis=0, tiled=True)  4.98 us
    ppermute x1, waiting for transfers between devices, body(): arrived = lax.ppermute(grads(1, dtype=jnp.bfloat16), 'section', across)  4.71 us
    pallas_call x1, Pallas kernels, pack(): pl.pallas_call(functools.partial(pack_kernel, per_half), out_shape=[jax.S...  4.12 us
    pallas_call x2, Pallas kernels, unit_grads(): pl.pallas_call(functools.partial(grads_kernel, which, per_half, owners, l...  3.38 us
    ppermute x1, starting transfers between devices, body(): arrived = lax.ppermute(grads(1, dtype=jnp.bfloat16), 'section', across)  2.72 us
    ppermute x3, starting transfers between devices, swapped(): return lax.ppermute(array, 'fsdp', [(i, i ^ apart) for i in range(size)])  2.53 us
  transfers between devices with their start and end apart: 5, of which 3 were waited for; matrix products, arithmetic and copies ran while one was open for 2% of the time, Pallas kernels for 12%

profile of v3, /device:TPU:0, one launch (start us, length us, event | category | flops | bytes accessed | tf_op | source)
XLA Modules:
  0.0 51.6 jit_solution(16895723761687417077)
XLA Ops:
  0.0 0.5 collective-permute-start
  0.5 4.1 %shard_map.64 = (bf16[8,2,2,128,128]{4,3,2,1,0:T(8,128)(2,1)}, s32[2,18]{1,0:T(2,128)}, s32[2,18]{1,0:T(2,128)}) custom-call(s32[1,2,20]{2,1,0:T(2,128)} %rows_ref.1, s32[1,2,20]{2,1,0:T(2,128)} %cols_ref.1, s32[1,2,4]{2,1,0:T(2,128)} %counts_ref.3, bf16[1,1,128,6144]{3,2,1,0:T(8,128)(2,1)} %down_ref.1, bf16[1,1,128,6144]{3,2,1,0:T(8,128)(2,1)} %up_ref.1), custom_call_target="tpu_custom_call" | custom-call | bytes 2097152 | tf_op jit(solution)/shard_map/pallas_call | solution.py:135
  4.6 0.0 copy-start.3
  4.6 5.0 %all-to-all-start = ((bf16[8,2,2,128,128]{4,3,2,1,0:T(8,128)(2,1)}), bf16[8,2,2,128,128]{4,3,2,1,0:T(8,128)(2,1)S(1)}, u32[]{:S(2)}, u32[]{:S(2)}) async-start(bf16[8,2,2,128,128]{4,3,2,1,0:T(8,128)(2,1)} %get-tuple-element.10), calls=%async_computation | async-start | bytes 2097152 | tf_op jit(solution)/shard_map/all_to_all | solution.py:371
  9.6 0.0 copy-start
  9.6 0.0 collective-permute-done
  9.6 0.0 copy-done.3
  9.6 1.2 %pad_maximum_fusion.near_ref = bf16[2,10,2,128,128]{4,3,2,1,0:T(8,128)(2,1)S(1)} fusion(bf16[2,5,2,128,128]{4,3,2,1,0:T(8,128)(2,1)} %collective-permute-done, bf16[2,5,2,128,128]{4,3,2,1,0:T(8,128)(2,1)S(1)} %bitcast.3), kind=kLoop, calls=%fused_computation | loop fusion | flops 655360 | bytes 2621440 | tf_op jit(solution)/shard_map/concatenate | solution.py:372
  10.8 0.0 copy-start.2
  10.8 0.0 copy-done
  10.8 0.6 %shard_map.65 = bf16[2,2,128,128]{3,2,1,0:T(8,128)(2,1)S(1)} custom-call(s32[2,18]{1,0:T(2,128)S(1)} %copy-done, bf16[2,10,2,128,128]{4,3,2,1,0:T(8,128)(2,1)S(1)} %pad_maximum_fusion.near_ref), custom_call_target="tpu_custom_call" | custom-call | bytes 300000 | tf_op jit(solution)/shard_map/pallas_call | solution.py:177
  11.4 2.1 %collective-permute-start.1 = (bf16[2,2,128,128]{3,2,1,0:T(8,128)(2,1)S(1)}, bf16[2,2,128,128]{3,2,1,0:T(8,128)(2,1)S(1)}, u32[]{:S(2)}, u32[]{:S(2)}) collective-permute-start(bf16[2,2,128,128]{3,2,1,0:T(8,128)(2,1)S(1)} %shard_map.65), channel_id=1, source_target_pairs={{0,2},{1,3},{2,0},{3,1},{4,6},{5,7},{6,4},{7,5},{8,10},{9,11},{10,... | collective-permute-start | bytes 393224 | tf_op jit(solution)/shard_map/ppermute | solution.py:157
  13.5 13.3 %collective-permute-done.1.far_ref = bf16[2,2,128,128]{3,2,1,0:T(8,128)(2,1)S(1)} collective-permute-done((bf16[2,2,128,128]{3,2,1,0:T(8,128)(2,1)S(1)}, bf16[2,2,128,128]{3,2,1,0:T(8,128)(2,1)S(1)}, u32[]{:S(2)}, u32[]{:S(2)}) %collective-permute-start.1) | collective-permute-done | bytes 131104 | tf_op jit(solution)/shard_map/ppermute | solution.py:157
  26.8 0.0 all-to-all-done.x_ref
  26.8 0.0 copy-done.2
  26.9 1.7 %shard_map.67 = bf16[2,2,128,128]{3,2,1,0:T(8,128)(2,1)S(1)} custom-call(s32[2,18]{1,0:T(2,128)S(1)} %copy-done, s32[2,18]{1,0:T(2,128)S(1)} %copy-done.2, bf16[8,2,2,128,128]{4,3,2,1,0:T(8,128)(2,1)S(1)} %all-to-all-done.x_ref, bf16[2,10,2,128,128]{4,3,2,1,0:T(8,128)(2,1)S(1)} %pad_maximum_fusion.near_ref, ...), custom_call_target="tpu_custom_call" | custom-call | flops 335544320 | bytes 524288 | tf_op jit(solution)/shard_map/pallas_call | solution.py:275
  28.6 2.7 %collective-permute-start.2 = (bf16[2,2,128,128]{3,2,1,0:T(8,128)(2,1)S(1)}, bf16[2,2,128,128]{3,2,1,0:T(8,128)(2,1)S(1)}, u32[]{:S(2)}, u32[]{:S(2)}) collective-permute-start(bf16[2,2,128,128]{3,2,1,0:T(8,128)(2,1)S(1)} %shard_map.67), channel_id=1, source_target_pairs={{0,16},{8,24},{16,0},{24,8},{1,17},{9,25},{17,1},{25,9},{2,18},{10... | collective-permute-start | bytes 393224 | tf_op jit(solution)/shard_map/ppermute | solution.py:378
  31.3 1.7 %shard_map.66.own_ref = f32[2,2,128,128]{3,2,1,0:T(8,128)S(1)} custom-call(s32[2,18]{1,0:T(2,128)S(1)} %copy-done, s32[2,18]{1,0:T(2,128)S(1)} %copy-done.2, bf16[8,2,2,128,128]{4,3,2,1,0:T(8,128)(2,1)S(1)} %all-to-all-done.x_ref, bf16[2,10,2,128,128]{4,3,2,1,0:T(8,128)(2,1)S(1)} %pad_maximum_fusion.near_ref, ...), custom_call_target="tpu_custom_call" | custom-call | flops 335544320 | bytes 524288 | tf_op jit(solution)/shard_map/pallas_call | solution.py:275
  33.0 0.0 copy-start.1
  33.0 4.7 %collective-permute-done.2.arrived_ref = bf16[2,2,128,128]{3,2,1,0:T(8,128)(2,1)S(1)} collective-permute-done((bf16[2,2,128,128]{3,2,1,0:T(8,128)(2,1)S(1)}, bf16[2,2,128,128]{3,2,1,0:T(8,128)(2,1)S(1)}, u32[]{:S(2)}, u32[]{:S(2)}) %collective-permute-start.2) | collective-permute-done | bytes 131104 | tf_op jit(solution)/shard_map/ppermute | solution.py:378
  37.7 10.5 %all_to_all.10.same_ref = bf16[4,2,2,128,128]{4,3,2,1,0:T(8,128)(2,1)S(1)} all-to-all(bf16[4,2,2,128,128]{4,3,2,1,0:T(8,128)(2,1)S(1)} %shard_map.68), channel_id=1, replica_groups={{0,2,4,6},{1,3,5,7},{8,10,12,14},{9,11,13,15},{16,18,20,22},{17,19,21,2..., dimensions={0} | all-to-all | bytes 1048576 | tf_op jit(solution)/shard_map/all_to_all | solution.py:383
  48.2 0.0 collective-permute-start.3
  48.2 1.9 %collective-permute-done.3.other_ref = bf16[4,2,2,128,128]{4,3,2,1,0:T(8,128)(2,1)S(1)} collective-permute-done((bf16[4,2,2,128,128]{4,3,2,1,0:T(8,128)(2,1)S(1)}, bf16[4,2,2,128,128]{4,3,2,1,0:T(8,128)(2,1)S(1)}, u32[]{:S(2)}, u32[]{:S(2)}) %collective-permute-start.3) | collective-permute-done | bytes 524320 | tf_op jit(solution)/shard_map/ppermute | solution.py:157
  50.1 0.0 copy-done.1
  50.1 1.5 %shard_map.69 = bf16[5,2,128,128]{3,2,1,0:T(8,128)(2,1)} custom-call(s32[2,18]{1,0:T(2,128)S(1)} %copy-done, s32[1,2,4]{2,1,0:T(2,128)S(1)} %copy-done.1, bf16[4,2,2,128,128]{4,3,2,1,0:T(8,128)(2,1)S(1)} %all_to_all.10.same_ref, bf16[4,2,2,128,128]{4,3,2,1,0:T(8,128)(2,1)S(1)} %collective-permute-done.3.other_ref), custom_call_target="tpu_custom_call" | custom-call | bytes 1000000 | tf_op jit(solution)/shard_map/pallas_call | solution.py:346
  (1 shorter events, 0.0 us)
Async XLA Ops:
  0.0 9.6 %collective-permute-start = (bf16[2,5,2,128,128]{4,3,2,1,0:T(8,128)(2,1)}, bf16[2,5,2,128,128]{4,3,2,1,0:T(8,128)(2,1)}, u32[]{:S(2)}, u32[]{:S(2)}) collective-permute-start(bf16[2,5,2,128,128]{4,3,2,1,0:T(8,128)(2,1)} %bitcast.2), channel_id=1, source_target_pairs={{0,1},{1,0},{2,3},{3,2},{4,5},{5,4},{6,7},{7,6},{8,9},{9,8},{10,11... | collective-permute-start | bytes 1966088 | tf_op jit(solution)/shard_map/ppermute | solution.py:157
  4.6 5.0 %copy-start.3 = (bf16[1,2,5,2,128,128]{5,4,3,2,1,0:T(8,128)(2,1)S(1)}, bf16[1,2,5,2,128,128]{5,4,3,2,1,0:T(8,128)(2,1)}, u32[]{:S(2)}) copy-start(bf16[1,2,5,2,128,128]{5,4,3,2,1,0:T(8,128)(2,1)} %param.8) | copy-start | bytes 1966084
  4.6 22.3 %all-to-all-start = ((bf16[8,2,2,128,128]{4,3,2,1,0:T(8,128)(2,1)}), bf16[8,2,2,128,128]{4,3,2,1,0:T(8,128)(2,1)S(1)}, u32[]{:S(2)}, u32[]{:S(2)}) async-start(bf16[8,2,2,128,128]{4,3,2,1,0:T(8,128)(2,1)} %get-tuple-element.10), calls=%async_computation | async-start | bytes 2097152 | tf_op jit(solution)/shard_map/all_to_all | solution.py:371
  9.6 1.2 %copy-start = (s32[2,18]{1,0:T(2,128)S(1)}, s32[2,18]{1,0:T(2,128)}, u32[]{:S(2)}) copy-start(s32[2,18]{1,0:T(2,128)} %get-tuple-element.8.order_ref) | copy-start | bytes 436
  10.8 16.0 %copy-start.2 = (s32[2,18]{1,0:T(2,128)S(1)}, s32[2,18]{1,0:T(2,128)}, u32[]{:S(2)}) copy-start(s32[2,18]{1,0:T(2,128)} %get-tuple-element.9.flags_ref) | copy-start | bytes 436
  11.4 15.4 %collective-permute-start.1 = (bf16[2,2,128,128]{3,2,1,0:T(8,128)(2,1)S(1)}, bf16[2,2,128,128]{3,2,1,0:T(8,128)(2,1)S(1)}, u32[]{:S(2)}, u32[]{:S(2)}) collective-permute-start(bf16[2,2,128,128]{3,2,1,0:T(8,128)(2,1)S(1)} %shard_map.65), channel_id=1, source_target_pairs={{0,2},{1,3},{2,0},{3,1},{4,6},{5,7},{6,4},{7,5},{8,10},{9,11},{10,... | collective-permute-start | bytes 393224 | tf_op jit(solution)/shard_map/ppermute | solution.py:157
  28.6 9.1 %collective-permute-start.2 = (bf16[2,2,128,128]{3,2,1,0:T(8,128)(2,1)S(1)}, bf16[2,2,128,128]{3,2,1,0:T(8,128)(2,1)S(1)}, u32[]{:S(2)}, u32[]{:S(2)}) collective-permute-start(bf16[2,2,128,128]{3,2,1,0:T(8,128)(2,1)S(1)} %shard_map.67), channel_id=1, source_target_pairs={{0,16},{8,24},{16,0},{24,8},{1,17},{9,25},{17,1},{25,9},{2,18},{10... | collective-permute-start | bytes 393224 | tf_op jit(solution)/shard_map/ppermute | solution.py:378
  33.0 17.2 %copy-start.1 = (s32[1,2,4]{2,1,0:T(2,128)S(1)}, s32[1,2,4]{2,1,0:T(2,128)}, u32[]{:S(2)}) copy-start(s32[1,2,4]{2,1,0:T(2,128)} %counts_ref.3) | copy-start | bytes 100
  48.2 1.9 %collective-permute-start.3 = (bf16[4,2,2,128,128]{4,3,2,1,0:T(8,128)(2,1)S(1)}, bf16[4,2,2,128,128]{4,3,2,1,0:T(8,128)(2,1)S(1)}, u32[]{:S(2)}, u32[]{:S(2)}) collective-permute-start(bf16[4,2,2,128,128]{4,3,2,1,0:T(8,128)(2,1)S(1)} %all_to_all.10.same_ref), channel_id=1, source_target_pairs={{0,1},{1,0},{2,3},{3,2},{4,5},{5,4},{6,7},{7,6},{8,9},{9,8},{10,11... | collective-permute-start | bytes 1572872 | tf_op jit(solution)/shard_map/ppermute | solution.py:157

commit v4 on v3

--- a/solution.py
+++ b/solution.py
@@ -163,22 +163,28 @@
     return other + slot - owner * per_owner
 
 
-def far_kernel(per_half, order_ref, near_ref, out_ref):
+def far_kernel(per_half, order_ref, near_ref, own_ref, partner_ref):
     per_owner, owners = near_ref.shape[1] // CORES, 2 * CORES
     unit = unit_here(per_half, owners)
     asker = jnp.where(unit < per_half, unit + per_half, unit - per_half)
-    for which in range(2):
-        slot = jnp.maximum(order_ref[which, 2 * asker + 1], 0)
-        out_ref[which] = near_ref[which, near_at(slot, per_owner)]
-
-
-def far_weights(near, order, per_half):
+    at = [
+        near_at(jnp.maximum(order_ref[which, 2 * asker + 1], 0), per_owner) for which in range(2)
+    ]
+    for half in range(own_ref.shape[0]):
+        own_ref[half] = near_ref[0, at[0]]
+    partner_ref[0] = near_ref[1, at[1]]
+
+
+def far_weights(near, order, per_half, halves):
     vmem = pl.BlockSpec(memory_space=pltpu.VMEM)
     return pl.pallas_call(
         functools.partial(far_kernel, per_half),
-        out_shape=jax.ShapeDtypeStruct(near.shape[:1] + near.shape[2:], near.dtype),
+        out_shape=[
+            jax.ShapeDtypeStruct((halves,) + near.shape[2:], near.dtype),
+            jax.ShapeDtypeStruct((1,) + near.shape[2:], near.dtype),
+        ],
         in_specs=[pl.BlockSpec(memory_space=pltpu.SMEM), vmem],
-        out_specs=vmem,
+        out_specs=[vmem, vmem],
         compiler_params=IN_VMEM,
         cost_estimate=pl.CostEstimate(flops=0, bytes_accessed=300_000, transcendentals=0),
     )(order, near)
@@ -208,7 +214,7 @@
 
         @pl.when(jnp.logical_not(near))
         def _():
-            w_unit[i] = far_ref[which]
+            w_unit[i] = far_ref[0 if far_ref.shape[0] == 1 else 1 - half]
 
     together = min(SOURCES_AT_ONCE, sources)
     steps = sources // together
@@ -370,13 +376,20 @@
     packed, order, flags = pack(x_down, x_up, tile_rows, tile_cols, counts, per_half, places)
     blocks = lax.all_to_all(packed, PLANE, split_axis=0, concat_axis=0, tiled=True)
     near = jnp.concatenate([w_tiles[0], swapped(w_tiles[0], 1)], axis=1)
-    far = swapped(far_weights(near, order, per_half), CORES)
+    halves = owners // CORES
+    far_own, far_partner = far_weights(near, order, per_half, halves)
+    pairs = [[half * CORES + core for half in range(halves)] for core in range(CORES)]
+    far_own = lax.all_to_all(
+        far_own, "fsdp", split_axis=0, concat_axis=0, axis_index_groups=pairs, tiled=True
+    )
+    far_partner = swapped(far_partner, CORES)
     grads = functools.partial(
-        unit_grads, blocks=blocks, near=near, far=far, order=order, flags=flags,
+        unit_grads, blocks=blocks, near=near, order=order, flags=flags,
         per_half=per_half, owners=owners, loss_scale=loss_scale,
     )
-    arrived = lax.ppermute(grads(1, dtype=jnp.bfloat16), "section", across)
-    mine = add(grads(0, dtype=jnp.float32), arrived, places // CORES)
+    partner = grads(1, far=far_partner, dtype=jnp.bfloat16)
+    arrived = lax.ppermute(partner, "section", across)
+    mine = add(grads(0, far=far_own, dtype=jnp.float32), arrived, places // CORES)
     same_core = [
         [place for place in range(places) if place % CORES == core] for core in range(CORES)
     ]

time: 52 us -> 52.4 us (level)
  blocking collectives: 10.5 us -> 17.3 us
  waiting for transfers between devices: 20 us -> 14.5 us
  other arithmetic: 1.21 us -> 0.12 us
    all_to_all x0 -> x1, blocking collectives: none -> 6.84 us  [body(): lax.all_to_all(far_own, 'fsdp', split_axis=0, concat_axis=0, axis_index_g...]
    ppermute x1, waiting for transfers between devices: 4.71 us -> 0.01 us  [body(): arrived = lax.ppermute(partner, 'section', across)]
    concatenate x1, other arithmetic: 1.21 us -> 0.12 us  [body(): near = jnp.concatenate([w_tiles[0], swapped(w_tiles[0], 1)], axis=1)]
    ppermute x3, waiting for transfers between devices: 15.2 us -> 14.5 us  [swapped(): return lax.ppermute(array, 'fsdp', [(i, i ^ apart) for i in range(size)])]
  transfers between devices with their start and end apart: 5 -> 5, of which waited for: 3 -> 3; matrix products, arithmetic and copies ran while one was open for 2% -> 0% of each run, Pallas kernels for 12% -> 4%
where the time goes in v4:
time: 52.4 us; the launch traced here: 52.2 us
  blocking collectives  17.3 us (33%)
  waiting for transfers between devices  14.5 us (28%)
  starting transfers between devices  10.5 us (20%)
  Pallas kernels  9.63 us (18%)
    ppermute x3, waiting for transfers between devices, swapped(): return lax.ppermute(array, 'fsdp', [(i, i ^ apart) for i in range(size)])  14.5 us
    all_to_all x1, blocking collectives, body(): lax.all_to_all(mine, PLANE, split_axis=0, concat_axis=0, axis_index_group...  10.5 us
    all_to_all x1, blocking collectives, body(): lax.all_to_all(far_own, 'fsdp', split_axis=0, concat_axis=0, axis_index_g...  6.84 us
    all_to_all x1, starting transfers between devices, body(): lax.all_to_all(packed, PLANE, split_axis=0, concat_axis=0, tiled=True)  5.31 us
    pallas_call x1, Pallas kernels, pack(): pl.pallas_call(functools.partial(pack_kernel, per_half), out_shape=[jax.S...  4.12 us
    pallas_call x2, Pallas kernels, unit_grads(): pl.pallas_call(functools.partial(grads_kernel, which, per_half, owners, l...  3.38 us
    ppermute x1, starting transfers between devices, body(): arrived = lax.ppermute(partner, 'section', across)  2.65 us
    ppermute x3, starting transfers between devices, swapped(): return lax.ppermute(array, 'fsdp', [(i, i ^ apart) for i in range(size)])  2.51 us
  transfers between devices with their start and end apart: 5, of which 3 were waited for; matrix products, arithmetic and copies ran while one was open for 0% of the time, Pallas kernels for 4%

profile of v4, /device:TPU:0, one launch (start us, length us, event | category | flops | bytes accessed | tf_op | source)
XLA Modules:
  0.0 52.2 jit_solution(5739787410374404373)
XLA Ops:
  0.0 4.1 %shard_map.64 = (bf16[8,2,2,128,128]{4,3,2,1,0:T(8,128)(2,1)}, s32[2,18]{1,0:T(2,128)}, s32[2,18]{1,0:T(2,128)}) custom-call(s32[1,2,20]{2,1,0:T(2,128)} %rows_ref.1, s32[1,2,20]{2,1,0:T(2,128)} %cols_ref.1, s32[1,2,4]{2,1,0:T(2,128)} %counts_ref.3, bf16[1,1,128,6144]{3,2,1,0:T(8,128)(2,1)} %down_ref.1, bf16[1,1,128,6144]{3,2,1,0:T(8,128)(2,1)} %up_ref.1), custom_call_target="tpu_custom_call" | custom-call | bytes 2097152 | tf_op jit(solution)/shard_map/pallas_call | solution.py:135
  4.1 0.0 copy-start.3
  4.1 5.3 %all-to-all-start = ((bf16[8,2,2,128,128]{4,3,2,1,0:T(8,128)(2,1)}), bf16[8,2,2,128,128]{4,3,2,1,0:T(8,128)(2,1)S(1)}, u32[]{:S(2)}, u32[]{:S(2)}) async-start(bf16[8,2,2,128,128]{4,3,2,1,0:T(8,128)(2,1)} %get-tuple-element.12), calls=%async_computation | async-start | bytes 2097152 | tf_op jit(solution)/shard_map/all_to_all | solution.py:377
  9.5 0.0 copy-done.3
  9.5 0.0 copy-start
  9.5 0.6 %collective-permute-start = (bf16[2,5,2,128,128]{4,3,2,1,0:T(8,128)(2,1)S(1)}, bf16[2,5,2,128,128]{4,3,2,1,0:T(8,128)(2,1)S(1)}, u32[]{:S(2)}, u32[]{:S(2)}) collective-permute-start(bf16[2,5,2,128,128]{4,3,2,1,0:T(8,128)(2,1)S(1)} %bitcast.2), channel_id=1, source_target_pairs={{0,1},{1,0},{2,3},{3,2},{4,5},{5,4},{6,7},{7,6},{8,9},{9,8},{10,11... | collective-permute-start | bytes 1966088 | tf_op jit(solution)/shard_map/ppermute | solution.py:157
  10.0 1.7 %collective-permute-done = bf16[2,5,2,128,128]{4,3,2,1,0:T(8,128)(2,1)S(1)} collective-permute-done((bf16[2,5,2,128,128]{4,3,2,1,0:T(8,128)(2,1)S(1)}, bf16[2,5,2,128,128]{4,3,2,1,0:T(8,128)(2,1)S(1)}, u32[]{:S(2)}, u32[]{:S(2)}) %collective-permute-start) | collective-permute-done | bytes 655392 | tf_op jit(solution)/shard_map/ppermute | solution.py:157
  11.8 0.1 pad_maximum_fusion.near_ref
  11.9 0.0 copy-start.2
  11.9 0.0 copy-done
  11.9 0.6 %shard_map.65 = (bf16[2,2,128,128]{3,2,1,0:T(8,128)(2,1)S(1)}, bf16[1,2,128,128]{3,2,1,0:T(8,128)(2,1)S(1)}) custom-call(s32[2,18]{1,0:T(2,128)S(1)} %copy-done, bf16[2,10,2,128,128]{4,3,2,1,0:T(8,128)(2,1)S(1)} %pad_maximum_fusion.near_ref), custom_call_target="tpu_custom_call" | custom-call | bytes 300000 | tf_op jit(solution)/shard_map/pallas_call | solution.py:180
  12.5 2.0 %collective-permute-start.1 = (bf16[1,2,128,128]{3,2,1,0:T(8,128)(2,1)S(1)}, bf16[1,2,128,128]{3,2,1,0:T(8,128)(2,1)S(1)}, u32[]{:S(2)}, u32[]{:S(2)}) collective-permute-start(bf16[1,2,128,128]{3,2,1,0:T(8,128)(2,1)S(1)} %get-tuple-element.14), channel_id=1, source_target_pairs={{0,2},{1,3},{2,0},{3,1},{4,6},{5,7},{6,4},{7,5},{8,10},{9,11},{10,... | collective-permute-start | bytes 196616 | tf_op jit(solution)/shard_map/ppermute | solution.py:157
  14.5 10.9 %collective-permute-done.1.far_ref = bf16[1,2,128,128]{3,2,1,0:T(8,128)(2,1)S(1)} collective-permute-done((bf16[1,2,128,128]{3,2,1,0:T(8,128)(2,1)S(1)}, bf16[1,2,128,128]{3,2,1,0:T(8,128)(2,1)S(1)}, u32[]{:S(2)}, u32[]{:S(2)}) %collective-permute-start.1) | collective-permute-done | bytes 65568 | tf_op jit(solution)/shard_map/ppermute | solution.py:157
  25.3 0.0 all-to-all-done.x_ref
  25.3 0.0 copy-done.2
  25.3 1.7 %shard_map.67 = bf16[2,2,128,128]{3,2,1,0:T(8,128)(2,1)S(1)} custom-call(s32[2,18]{1,0:T(2,128)S(1)} %copy-done, s32[2,18]{1,0:T(2,128)S(1)} %copy-done.2, bf16[8,2,2,128,128]{4,3,2,1,0:T(8,128)(2,1)S(1)} %all-to-all-done.x_ref, bf16[2,10,2,128,128]{4,3,2,1,0:T(8,128)(2,1)S(1)} %pad_maximum_fusion.near_ref, ...), custom_call_target="tpu_custom_call" | custom-call | flops 335544320 | bytes 524288 | tf_op jit(solution)/shard_map/pallas_call | solution.py:281
  27.0 2.7 %collective-permute-start.2 = (bf16[2,2,128,128]{3,2,1,0:T(8,128)(2,1)S(1)}, bf16[2,2,128,128]{3,2,1,0:T(8,128)(2,1)S(1)}, u32[]{:S(2)}, u32[]{:S(2)}) collective-permute-start(bf16[2,2,128,128]{3,2,1,0:T(8,128)(2,1)S(1)} %shard_map.67), channel_id=1, source_target_pairs={{0,16},{8,24},{16,0},{24,8},{1,17},{9,25},{17,1},{25,9},{2,18},{10... | collective-permute-start | bytes 393224 | tf_op jit(solution)/shard_map/ppermute | solution.py:391
  29.7 6.8 %all_to_all.15.far_ref = bf16[2,2,128,128]{3,2,1,0:T(8,128)(2,1)S(1)} all-to-all(bf16[2,2,128,128]{3,2,1,0:T(8,128)(2,1)S(1)} %get-tuple-element.13), channel_id=1, replica_groups={{0,2},{1,3},{4,6},{5,7},{8,10},{9,11},{12,14},{13,15},{16,18},{17,19},{..., dimensions={0} | all-to-all | bytes 262144 | tf_op jit(solution)/shard_map/all_to_all | solution.py:382
  36.5 1.7 %shard_map.66.own_ref = f32[2,2,128,128]{3,2,1,0:T(8,128)S(1)} custom-call(s32[2,18]{1,0:T(2,128)S(1)} %copy-done, s32[2,18]{1,0:T(2,128)S(1)} %copy-done.2, bf16[8,2,2,128,128]{4,3,2,1,0:T(8,128)(2,1)S(1)} %all-to-all-done.x_ref, bf16[2,10,2,128,128]{4,3,2,1,0:T(8,128)(2,1)S(1)} %pad_maximum_fusion.near_ref, bf16[2,2,128,128]{3,2,1,0:T(8,128)(2,1)S(1)} %all_to_all.15.far_ref), custom_call_target="tpu_custom_call" | custom-call | flops 335544320 | bytes 524288 | tf_op jit(solution)/shard_map/pallas_call | solution.py:281
  38.2 0.0 copy-start.1
  38.2 0.0 collective-permute-done.2.arrived_ref
  38.3 10.5 %all_to_all.16.same_ref = bf16[4,2,2,128,128]{4,3,2,1,0:T(8,128)(2,1)S(1)} all-to-all(bf16[4,2,2,128,128]{4,3,2,1,0:T(8,128)(2,1)S(1)} %shard_map.68), channel_id=1, replica_groups={{0,2,4,6},{1,3,5,7},{8,10,12,14},{9,11,13,15},{16,18,20,22},{17,19,21,2..., dimensions={0} | all-to-all | bytes 1048576 | tf_op jit(solution)/shard_map/all_to_all | solution.py:396
  48.8 0.0 collective-permute-start.3
  48.8 1.9 %collective-permute-done.3.other_ref = bf16[4,2,2,128,128]{4,3,2,1,0:T(8,128)(2,1)S(1)} collective-permute-done((bf16[4,2,2,128,128]{4,3,2,1,0:T(8,128)(2,1)S(1)}, bf16[4,2,2,128,128]{4,3,2,1,0:T(8,128)(2,1)S(1)}, u32[]{:S(2)}, u32[]{:S(2)}) %collective-permute-start.3) | collective-permute-done | bytes 524320 | tf_op jit(solution)/shard_map/ppermute | solution.py:157
  50.7 0.0 copy-done.1
  50.7 1.5 %shard_map.69 = bf16[5,2,128,128]{3,2,1,0:T(8,128)(2,1)} custom-call(s32[2,18]{1,0:T(2,128)S(1)} %copy-done, s32[1,2,4]{2,1,0:T(2,128)S(1)} %copy-done.1, bf16[4,2,2,128,128]{4,3,2,1,0:T(8,128)(2,1)S(1)} %all_to_all.16.same_ref, bf16[4,2,2,128,128]{4,3,2,1,0:T(8,128)(2,1)S(1)} %collective-permute-done.3.other_ref), custom_call_target="tpu_custom_call" | custom-call | bytes 1000000 | tf_op jit(solution)/shard_map/pallas_call | solution.py:352
  (1 shorter events, 0.0 us)
Async XLA Ops:
  4.1 5.3 %copy-start.3 = (bf16[1,2,5,2,128,128]{5,4,3,2,1,0:T(8,128)(2,1)S(1)}, bf16[1,2,5,2,128,128]{5,4,3,2,1,0:T(8,128)(2,1)}, u32[]{:S(2)}) copy-start(bf16[1,2,5,2,128,128]{5,4,3,2,1,0:T(8,128)(2,1)} %param.8) | copy-start | bytes 1966084
  4.1 21.2 %all-to-all-start = ((bf16[8,2,2,128,128]{4,3,2,1,0:T(8,128)(2,1)}), bf16[8,2,2,128,128]{4,3,2,1,0:T(8,128)(2,1)S(1)}, u32[]{:S(2)}, u32[]{:S(2)}) async-start(bf16[8,2,2,128,128]{4,3,2,1,0:T(8,128)(2,1)} %get-tuple-element.12), calls=%async_computation | async-start | bytes 2097152 | tf_op jit(solution)/shard_map/all_to_all | solution.py:377
  9.5 2.4 %copy-start = (s32[2,18]{1,0:T(2,128)S(1)}, s32[2,18]{1,0:T(2,128)}, u32[]{:S(2)}) copy-start(s32[2,18]{1,0:T(2,128)} %get-tuple-element.10.order_ref) | copy-start | bytes 436
  9.5 2.3 %collective-permute-start = (bf16[2,5,2,128,128]{4,3,2,1,0:T(8,128)(2,1)S(1)}, bf16[2,5,2,128,128]{4,3,2,1,0:T(8,128)(2,1)S(1)}, u32[]{:S(2)}, u32[]{:S(2)}) collective-permute-start(bf16[2,5,2,128,128]{4,3,2,1,0:T(8,128)(2,1)S(1)} %bitcast.2), channel_id=1, source_target_pairs={{0,1},{1,0},{2,3},{3,2},{4,5},{5,4},{6,7},{7,6},{8,9},{9,8},{10,11... | collective-permute-start | bytes 1966088 | tf_op jit(solution)/shard_map/ppermute | solution.py:157
  11.9 13.5 %copy-start.2 = (s32[2,18]{1,0:T(2,128)S(1)}, s32[2,18]{1,0:T(2,128)}, u32[]{:S(2)}) copy-start(s32[2,18]{1,0:T(2,128)} %get-tuple-element.11.flags_ref) | copy-start | bytes 436
  12.5 12.8 %collective-permute-start.1 = (bf16[1,2,128,128]{3,2,1,0:T(8,128)(2,1)S(1)}, bf16[1,2,128,128]{3,2,1,0:T(8,128)(2,1)S(1)}, u32[]{:S(2)}, u32[]{:S(2)}) collective-permute-start(bf16[1,2,128,128]{3,2,1,0:T(8,128)(2,1)S(1)} %get-tuple-element.14), channel_id=1, source_target_pairs={{0,2},{1,3},{2,0},{3,1},{4,6},{5,7},{6,4},{7,5},{8,10},{9,11},{10,... | collective-permute-start | bytes 196616 | tf_op jit(solution)/shard_map/ppermute | solution.py:157
  27.0 11.2 %collective-permute-start.2 = (bf16[2,2,128,128]{3,2,1,0:T(8,128)(2,1)S(1)}, bf16[2,2,128,128]{3,2,1,0:T(8,128)(2,1)S(1)}, u32[]{:S(2)}, u32[]{:S(2)}) collective-permute-start(bf16[2,2,128,128]{3,2,1,0:T(8,128)(2,1)S(1)} %shard_map.67), channel_id=1, source_target_pairs={{0,16},{8,24},{16,0},{24,8},{1,17},{9,25},{17,1},{25,9},{2,18},{10... | collective-permute-start | bytes 393224 | tf_op jit(solution)/shard_map/ppermute | solution.py:391
  38.2 12.5 %copy-start.1 = (s32[1,2,4]{2,1,0:T(2,128)S(1)}, s32[1,2,4]{2,1,0:T(2,128)}, u32[]{:S(2)}) copy-start(s32[1,2,4]{2,1,0:T(2,128)} %counts_ref.3) | copy-start | bytes 100
  48.8 1.9 %collective-permute-start.3 = (bf16[4,2,2,128,128]{4,3,2,1,0:T(8,128)(2,1)S(1)}, bf16[4,2,2,128,128]{4,3,2,1,0:T(8,128)(2,1)S(1)}, u32[]{:S(2)}, u32[]{:S(2)}) collective-permute-start(bf16[4,2,2,128,128]{4,3,2,1,0:T(8,128)(2,1)S(1)} %all_to_all.16.same_ref), channel_id=1, source_target_pairs={{0,1},{1,0},{2,3},{3,2},{4,5},{5,4},{6,7},{7,6},{8,9},{9,8},{10,11... | collective-permute-start | bytes 1572872 | tf_op jit(solution)/shard_map/ppermute | solution.py:157

commit v5 on v3

--- a/solution.py
+++ b/solution.py
@@ -13,6 +13,7 @@
 SOURCES_AT_ONCE = 8
 COLUMNS = 192
 CORES = 2
+COUPLED = 64
 IN_VMEM = pltpu.CompilerParams(vmem_limit_bytes=16 * 1024 * 1024)
 
 tanh_scale = math.sqrt(2.0 / math.pi)
@@ -47,12 +48,13 @@
 
 
 def order_units(
-    cols_ref, counts_ref, which, slots, per_half, order_ref, flags_ref, first_ref, last_ref
+    cols_ref, counts_ref, which, slots, per_half, order_ref, first_ref, last_ref
 ):
     per_owner, middle, unused = slots // counts_ref.shape[2], slots // 2, 4 * per_half
-    for i in range(order_ref.shape[1]):
+    for i in range(unused):
         order_ref[which, i] = -1
-        flags_ref[which, i] = 0
+    for owner in range(counts_ref.shape[2]):
+        order_ref[which, unused + 2 + owner] = counts_ref[0, which, owner]
     cols = []
     for s in range(slots):
         living = counts_ref[0, which, s // per_owner] > s % per_owner
@@ -64,9 +66,8 @@
 
     def put(unit, slot_a, slot_b, coupled, really):
         at = jnp.where(really, 2 * unit, unused)
-        order_ref[which, at] = slot_a
+        order_ref[which, at] = slot_a + coupled * COUPLED
         order_ref[which, at + 1] = slot_b
-        flags_ref[which, at] = coupled
 
     count = lambda condition: jnp.where(condition, 1, 0)
     alone, mixed = [], []
@@ -98,53 +99,66 @@
         filled[1] = filled[1] + count(really & jnp.logical_not(room))
 
 
+def slot_in(order_ref, which, i):
+    return jnp.maximum(order_ref[which, i], 0) % COUPLED
+
+
 def pack_kernel(
     per_half, rows_ref, cols_ref, counts_ref, down_ref, up_ref,
-    out_ref, order_ref, flags_ref, first_ref, last_ref, sems,
+    out_ref, order_ref, held, zeros, first_ref, last_ref, in_sems, out_sems, zero_sem,
 ):
     slots, owners = cols_ref.shape[2], counts_ref.shape[2]
     places, units = out_ref.shape[0], 2 * per_half
-    copies = []
     used = [unit_place(unit, per_half, owners) for unit in range(units)]
+    arriving, leaving = [], []
     for which, x_ref in ((1, up_ref), (0, down_ref)):
-        order_units(
-            cols_ref, counts_ref, which, slots, per_half, order_ref, flags_ref, first_ref, last_ref
-        )
+        order_units(cols_ref, counts_ref, which, slots, per_half, order_ref, first_ref, last_ref)
         for i in range(2 * units):
-            row = rows_ref[0, which, jnp.maximum(order_ref[which, i], 0)]
+            row = rows_ref[0, which, slot_in(order_ref, which, i)]
             at = pl.multiple_of(row * TILE, TILE)
             copy = pltpu.make_async_copy(
-                x_ref.at[0, 0, :, pl.ds(at, TILE)],
-                out_ref.at[used[i // 2], which, i % 2],
-                sems.at[which, i],
+                x_ref.at[0, 0, :, pl.ds(at, TILE)], held.at[which, i], in_sems.at[which, i]
             )
             copy.start()
-            copies.append(copy)
+            arriving.append((which, i, copy))
+    for which, i, copy in arriving:
+        copy.wait()
+        onward = pltpu.make_async_copy(
+            held.at[which, i], out_ref.at[used[i // 2], which, i % 2], out_sems.at[which, i]
+        )
+        onward.start()
+        leaving.append(onward)
+    if places > units:
+        zeros[...] = jnp.zeros_like(zeros)
     for place in range(places):
         if place not in used:
-            out_ref[place] = jnp.zeros(out_ref.shape[1:], out_ref.dtype)
-    for copy in copies:
-        copy.wait()
+            empty = pltpu.make_async_copy(zeros, out_ref.at[place], zero_sem)
+            empty.start()
+            empty.wait()
+    for onward in leaving:
+        onward.wait()
 
 
 def pack(x_down, x_up, tile_rows, tile_cols, counts, per_half, places):
     rows, units = x_down.shape[2], 2 * per_half
     smem = pl.BlockSpec(memory_space=pltpu.SMEM)
-    vmem = pl.BlockSpec(memory_space=pltpu.VMEM)
     hbm = pl.BlockSpec(memory_space=pl.ANY)
     return pl.pallas_call(
         functools.partial(pack_kernel, per_half),
         out_shape=[
             jax.ShapeDtypeStruct((places, 2, 2, rows, TILE), x_down.dtype),
-            jax.ShapeDtypeStruct((2, 2 * units + 2), jnp.int32),
-            jax.ShapeDtypeStruct((2, 2 * units + 2), jnp.int32),
+            jax.ShapeDtypeStruct((2, 2 * units + 2 + counts.shape[2]), jnp.int32),
         ],
         in_specs=[smem, smem, smem, hbm, hbm],
-        out_specs=[vmem, smem, smem],
+        out_specs=[hbm, smem],
         scratch_shapes=[
+            pltpu.VMEM((2, 2 * units, rows, TILE), x_down.dtype),
+            pltpu.VMEM((2, 2, rows, TILE), x_down.dtype),
             pltpu.SMEM((COLUMNS + 1,), jnp.int32),
             pltpu.SMEM((COLUMNS + 1,), jnp.int32),
             pltpu.SemaphoreType.DMA((2, 2 * units)),
+            pltpu.SemaphoreType.DMA((2, 2 * units)),
+            pltpu.SemaphoreType.DMA,
         ],
         cost_estimate=pl.CostEstimate(
             flops=0, bytes_accessed=16 * units * rows * TILE, transcendentals=0
@@ -168,7 +182,7 @@
     unit = unit_here(per_half, owners)
     asker = jnp.where(unit < per_half, unit + per_half, unit - per_half)
     for which in range(2):
-        slot = jnp.maximum(order_ref[which, 2 * asker + 1], 0)
+        slot = slot_in(order_ref, which, 2 * asker + 1)
         out_ref[which] = near_ref[which, near_at(slot, per_owner)]
 
 
@@ -191,7 +205,7 @@
 
 
 def grads_kernel(
-    which, per_half, owners, loss_scale, order_ref, flags_ref, x_ref, near_ref, far_ref, out_ref,
+    which, per_half, owners, loss_scale, order_ref, x_ref, near_ref, far_ref, out_ref,
     w_unit, first_sum, second_sum,
 ):
     sources, _, _, rows, _ = x_ref.shape
@@ -199,7 +213,7 @@
     unit = unit_here(per_half, owners)
     half = lax.axis_index("fsdp") // CORES
     for i in range(2):
-        slot = jnp.maximum(order_ref[which, 2 * unit + i], 0)
+        slot = slot_in(order_ref, which, 2 * unit + i)
         near = slot // per_owner // CORES == half
 
         @pl.when(near)
@@ -219,7 +233,7 @@
     def sum_up(total_ref, where, term):
         total_ref[where] = total_ref[where] + term if steps > 1 else term
 
-    coupled = flags_ref[which, 2 * unit] == 1
+    coupled = order_ref[which, 2 * unit] >= COUPLED
 
     def read(step):
         at = step * together
@@ -268,14 +282,14 @@
         out_ref[i, 1] = second_sum[:, across].astype(out_ref.dtype)
 
 
-def unit_grads(which, blocks, near, far, order, flags, per_half, owners, loss_scale, dtype):
+def unit_grads(which, blocks, near, far, order, per_half, owners, loss_scale, dtype):
     sources, _, _, rows, _ = blocks.shape
     smem = pl.BlockSpec(memory_space=pltpu.SMEM)
     vmem = pl.BlockSpec(memory_space=pltpu.VMEM)
     return pl.pallas_call(
         functools.partial(grads_kernel, which, per_half, owners, loss_scale),
         out_shape=jax.ShapeDtypeStruct((2, 2, TILE, TILE), dtype),
-        in_specs=[smem, smem, vmem, vmem, vmem],
+        in_specs=[smem, vmem, vmem, vmem],
         out_specs=vmem,
         scratch_shapes=[
             pltpu.VMEM((2, 2, TILE, TILE), jnp.bfloat16),
@@ -288,7 +302,7 @@
             bytes_accessed=4 * sources * rows * TILE,
             transcendentals=2 * sources * rows * TILE,
         ),
-    )(order, flags, blocks, near, far)
+    )(order, blocks, near, far)
 
 
 def add_kernel(own_ref, arrived_ref, out_ref):
@@ -309,15 +323,15 @@
     )(own, arrived)
 
 
-def place_kernel(per_half, order_ref, counts_ref, same_ref, other_ref, out_ref, zeros, sems, zero_sems):
-    owner, owners = lax.axis_index("fsdp"), counts_ref.shape[2]
+def place_kernel(per_half, owners, order_ref, same_ref, other_ref, out_ref, zeros, sems, zero_sems):
+    owner = lax.axis_index("fsdp")
     per_owner = out_ref.shape[0]
     zeros[...] = jnp.zeros_like(zeros)
 
     def each(act):
         for i in range(4 * per_half):
-            at = order_ref[0, i] - owner * per_owner
-            mine = (at >= 0) & (at < per_owner)
+            at = slot_in(order_ref, 0, i) - owner * per_owner
+            mine = (order_ref[0, i] >= 0) & (at >= 0) & (at < per_owner)
             place = unit_place(i // 2, per_half, owners)
             near = owner % CORES == place % CORES
             for grads_ref, where in ((same_ref, near), (other_ref, jnp.logical_not(near))):
@@ -332,7 +346,7 @@
 
         for slot in range(per_owner):
 
-            @pl.when(counts_ref[0, 0, owner] <= slot)
+            @pl.when(order_ref[0, 4 * per_half + 2 + owner] <= slot)
             def _():
                 act(pltpu.make_async_copy(zeros, out_ref.at[slot], zero_sems.at[slot]))
 
@@ -340,13 +354,13 @@
     each(lambda copy: copy.wait())
 
 
-def place(same, other, order, counts, per_half, per_owner):
+def place(same, other, order, per_half, owners, per_owner):
     smem = pl.BlockSpec(memory_space=pltpu.SMEM)
     hbm = pl.BlockSpec(memory_space=pl.ANY)
     return pl.pallas_call(
-        functools.partial(place_kernel, per_half),
+        functools.partial(place_kernel, per_half, owners),
         out_shape=jax.ShapeDtypeStruct((per_owner,) + same.shape[2:], same.dtype),
-        in_specs=[smem, smem, hbm, hbm],
+        in_specs=[smem, hbm, hbm],
         out_specs=hbm,
         scratch_shapes=[
             pltpu.VMEM(same.shape[2:], same.dtype),
@@ -355,7 +369,7 @@
         ],
         compiler_params=IN_VMEM,
         cost_estimate=pl.CostEstimate(flops=0, bytes_accessed=1_000_000, transcendentals=0),
-    )(order, counts, same, other)
+    )(order, same, other)
 
 
 def body(x_down, x_up, w_tiles, tile_rows, tile_cols, counts):
@@ -367,12 +381,12 @@
     across = [(i, (i + sections // 2) % sections) for i in range(sections)]
     loss_scale = float(2 * rows_here * places) ** (-0.5)
 
-    packed, order, flags = pack(x_down, x_up, tile_rows, tile_cols, counts, per_half, places)
+    packed, order = pack(x_down, x_up, tile_rows, tile_cols, counts, per_half, places)
     blocks = lax.all_to_all(packed, PLANE, split_axis=0, concat_axis=0, tiled=True)
     near = jnp.concatenate([w_tiles[0], swapped(w_tiles[0], 1)], axis=1)
     far = swapped(far_weights(near, order, per_half), CORES)
     grads = functools.partial(
-        unit_grads, blocks=blocks, near=near, far=far, order=order, flags=flags,
+        unit_grads, blocks=blocks, near=near, far=far, order=order,
         per_half=per_half, owners=owners, loss_scale=loss_scale,
     )
     arrived = lax.ppermute(grads(1, dtype=jnp.bfloat16), "section", across)
@@ -384,7 +398,7 @@
         mine, PLANE, split_axis=0, concat_axis=0, axis_index_groups=same_core, tiled=True
     )
     other = swapped(same, 1)
-    return place(same, other, order, counts, per_half, slots // owners)[None]
+    return place(same, other, order, per_half, owners, slots // owners)[None]
 
 
 def solution(mesh):

time: 52 us -> 52.7 us (1.013)
  Pallas kernels: 9.62 us -> 10.2 us
    pallas_call x1, Pallas kernels: 4.12 us -> 4.7 us  [pack(): pl.pallas_call(functools.partial(pack_kernel, per_half), out_shape=[jax.S...]
  transfers between devices with their start and end apart: 5 -> 5, of which waited for: 3 -> 3; matrix products, arithmetic and copies ran while one was open for 2% -> 2% of each run, Pallas kernels for 12% -> 13%
where the time goes in v5:
time: 52.7 us; the launch traced here: 52.4 us
  waiting for transfers between devices  19.8 us (38%)
  blocking collectives  11 us (21%)
  Pallas kernels  10.2 us (19%)
  starting transfers between devices  10.1 us (19%)
  other arithmetic  1.21 us (2%)
    ppermute x3, waiting for transfers between devices, swapped(): return lax.ppermute(array, 'fsdp', [(i, i ^ apart) for i in range(size)])  15.2 us
    all_to_all x1, blocking collectives, body(): lax.all_to_all(mine, PLANE, split_axis=0, concat_axis=0, axis_index_group...  11 us
    all_to_all x1, starting transfers between devices, body(): lax.all_to_all(packed, PLANE, split_axis=0, concat_axis=0, tiled=True)  4.98 us
    pallas_call x1, Pallas kernels, pack(): pl.pallas_call(functools.partial(pack_kernel, per_half), out_shape=[jax.S...  4.7 us
    ppermute x1, waiting for transfers between devices, body(): arrived = lax.ppermute(grads(1, dtype=jnp.bfloat16), 'section', across)  4.52 us
    pallas_call x2, Pallas kernels, unit_grads(): pl.pallas_call(functools.partial(grads_kernel, which, per_half, owners, l...  3.37 us
    ppermute x1, starting transfers between devices, body(): arrived = lax.ppermute(grads(1, dtype=jnp.bfloat16), 'section', across)  2.59 us
    ppermute x3, starting transfers between devices, swapped(): return lax.ppermute(array, 'fsdp', [(i, i ^ apart) for i in range(size)])  2.53 us
  transfers between devices with their start and end apart: 5, of which 3 were waited for; matrix products, arithmetic and copies ran while one was open for 2% of the time, Pallas kernels for 13%

profile of v5, /device:TPU:0, one launch (start us, length us, event | category | flops | bytes accessed | tf_op | source)
XLA Modules:
  0.0 52.4 jit_solution(819156657195401188)
XLA Ops:
  0.0 0.5 collective-permute-start
  0.5 4.7 %shard_map.64 = (bf16[8,2,2,128,128]{4,3,2,1,0:T(8,128)(2,1)}, s32[2,22]{1,0:T(2,128)}) custom-call(s32[1,2,20]{2,1,0:T(2,128)} %rows_ref.1, s32[1,2,20]{2,1,0:T(2,128)} %cols_ref.1, s32[1,2,4]{2,1,0:T(2,128)} %counts_ref.1, bf16[1,1,128,6144]{3,2,1,0:T(8,128)(2,1)} %down_ref.1, bf16[1,1,128,6144]{3,2,1,0:T(8,128)(2,1)} %up_ref.1), custom_call_target="tpu_custom_call" | custom-call | bytes 2097152 | tf_op jit(solution)/shard_map/pallas_call | solution.py:146
  5.2 0.0 copy-start.1
  5.2 5.0 %all-to-all-start = ((bf16[8,2,2,128,128]{4,3,2,1,0:T(8,128)(2,1)}), bf16[8,2,2,128,128]{4,3,2,1,0:T(8,128)(2,1)S(1)}, u32[]{:S(2)}, u32[]{:S(2)}) async-start(bf16[8,2,2,128,128]{4,3,2,1,0:T(8,128)(2,1)} %get-tuple-element.8), calls=%async_computation | async-start | bytes 2097152 | tf_op jit(solution)/shard_map/all_to_all | solution.py:385
  10.2 0.0 copy-start
  10.2 0.0 collective-permute-done
  10.2 0.0 copy-done.1
  10.2 1.2 %pad_maximum_fusion.near_ref = bf16[2,10,2,128,128]{4,3,2,1,0:T(8,128)(2,1)S(1)} fusion(bf16[2,5,2,128,128]{4,3,2,1,0:T(8,128)(2,1)} %collective-permute-done, bf16[2,5,2,128,128]{4,3,2,1,0:T(8,128)(2,1)S(1)} %bitcast.3), kind=kLoop, calls=%fused_computation | loop fusion | flops 655360 | bytes 2621440 | tf_op jit(solution)/shard_map/concatenate | solution.py:386
  11.4 0.0 copy-done
  11.4 0.6 %shard_map.65 = bf16[2,2,128,128]{3,2,1,0:T(8,128)(2,1)S(1)} custom-call(s32[2,22]{1,0:T(2,128)S(1)} %copy-done, bf16[2,10,2,128,128]{4,3,2,1,0:T(8,128)(2,1)S(1)} %pad_maximum_fusion.near_ref), custom_call_target="tpu_custom_call" | custom-call | bytes 300000 | tf_op jit(solution)/shard_map/pallas_call | solution.py:191
  12.0 2.1 %collective-permute-start.1 = (bf16[2,2,128,128]{3,2,1,0:T(8,128)(2,1)S(1)}, bf16[2,2,128,128]{3,2,1,0:T(8,128)(2,1)S(1)}, u32[]{:S(2)}, u32[]{:S(2)}) collective-permute-start(bf16[2,2,128,128]{3,2,1,0:T(8,128)(2,1)S(1)} %shard_map.65), channel_id=1, source_target_pairs={{0,2},{1,3},{2,0},{3,1},{4,6},{5,7},{6,4},{7,5},{8,10},{9,11},{10,... | collective-permute-start | bytes 393224 | tf_op jit(solution)/shard_map/ppermute | solution.py:171
  14.1 13.3 %collective-permute-done.1.far_ref = bf16[2,2,128,128]{3,2,1,0:T(8,128)(2,1)S(1)} collective-permute-done((bf16[2,2,128,128]{3,2,1,0:T(8,128)(2,1)S(1)}, bf16[2,2,128,128]{3,2,1,0:T(8,128)(2,1)S(1)}, u32[]{:S(2)}, u32[]{:S(2)}) %collective-permute-start.1) | collective-permute-done | bytes 131104 | tf_op jit(solution)/shard_map/ppermute | solution.py:171
  27.4 0.0 all-to-all-done.x_ref
  27.4 1.7 %shard_map.67 = bf16[2,2,128,128]{3,2,1,0:T(8,128)(2,1)S(1)} custom-call(s32[2,22]{1,0:T(2,128)S(1)} %copy-done, bf16[8,2,2,128,128]{4,3,2,1,0:T(8,128)(2,1)S(1)} %all-to-all-done.x_ref, bf16[2,10,2,128,128]{4,3,2,1,0:T(8,128)(2,1)S(1)} %pad_maximum_fusion.near_ref, bf16[2,2,128,128]{3,2,1,0:T(8,128)(2,1)S(1)} %collective-permute-done.1.far_ref), custom_call_target="tpu_custom_call" | custom-call | flops 335544320 | bytes 524288 | tf_op jit(solution)/shard_map/pallas_call | solution.py:289
  29.1 2.6 %collective-permute-start.2 = (bf16[2,2,128,128]{3,2,1,0:T(8,128)(2,1)S(1)}, bf16[2,2,128,128]{3,2,1,0:T(8,128)(2,1)S(1)}, u32[]{:S(2)}, u32[]{:S(2)}) collective-permute-start(bf16[2,2,128,128]{3,2,1,0:T(8,128)(2,1)S(1)} %shard_map.67), channel_id=1, source_target_pairs={{0,16},{8,24},{16,0},{24,8},{1,17},{9,25},{17,1},{25,9},{2,18},{10... | collective-permute-start | bytes 393224 | tf_op jit(solution)/shard_map/ppermute | solution.py:392
  31.7 1.7 %shard_map.66.own_ref = f32[2,2,128,128]{3,2,1,0:T(8,128)S(1)} custom-call(s32[2,22]{1,0:T(2,128)S(1)} %copy-done, bf16[8,2,2,128,128]{4,3,2,1,0:T(8,128)(2,1)S(1)} %all-to-all-done.x_ref, bf16[2,10,2,128,128]{4,3,2,1,0:T(8,128)(2,1)S(1)} %pad_maximum_fusion.near_ref, bf16[2,2,128,128]{3,2,1,0:T(8,128)(2,1)S(1)} %collective-permute-done.1.far_ref), custom_call_target="tpu_custom_call" | custom-call | flops 335544320 | bytes 524288 | tf_op jit(solution)/shard_map/pallas_call | solution.py:289
  33.4 4.5 %collective-permute-done.2.arrived_ref = bf16[2,2,128,128]{3,2,1,0:T(8,128)(2,1)S(1)} collective-permute-done((bf16[2,2,128,128]{3,2,1,0:T(8,128)(2,1)S(1)}, bf16[2,2,128,128]{3,2,1,0:T(8,128)(2,1)S(1)}, u32[]{:S(2)}, u32[]{:S(2)}) %collective-permute-start.2) | collective-permute-done | bytes 131104 | tf_op jit(solution)/shard_map/ppermute | solution.py:392
  38.0 11.0 %all_to_all.10.same_ref = bf16[4,2,2,128,128]{4,3,2,1,0:T(8,128)(2,1)S(1)} all-to-all(bf16[4,2,2,128,128]{4,3,2,1,0:T(8,128)(2,1)S(1)} %shard_map.68), channel_id=1, replica_groups={{0,2,4,6},{1,3,5,7},{8,10,12,14},{9,11,13,15},{16,18,20,22},{17,19,21,2..., dimensions={0} | all-to-all | bytes 1048576 | tf_op jit(solution)/shard_map/all_to_all | solution.py:397
  48.9 0.0 collective-permute-start.3
  48.9 1.9 %collective-permute-done.3.other_ref = bf16[4,2,2,128,128]{4,3,2,1,0:T(8,128)(2,1)S(1)} collective-permute-done((bf16[4,2,2,128,128]{4,3,2,1,0:T(8,128)(2,1)S(1)}, bf16[4,2,2,128,128]{4,3,2,1,0:T(8,128)(2,1)S(1)}, u32[]{:S(2)}, u32[]{:S(2)}) %collective-permute-start.3) | collective-permute-done | bytes 524320 | tf_op jit(solution)/shard_map/ppermute | solution.py:171
  50.9 1.5 %shard_map.69 = bf16[5,2,128,128]{3,2,1,0:T(8,128)(2,1)} custom-call(s32[2,22]{1,0:T(2,128)S(1)} %copy-done, bf16[4,2,2,128,128]{4,3,2,1,0:T(8,128)(2,1)S(1)} %all_to_all.10.same_ref, bf16[4,2,2,128,128]{4,3,2,1,0:T(8,128)(2,1)S(1)} %collective-permute-done.3.other_ref), custom_call_target="tpu_custom_call" | custom-call | bytes 1000000 | tf_op jit(solution)/shard_map/pallas_call | solution.py:360
  (1 shorter events, 0.0 us)
Async XLA Ops:
  0.0 10.2 %collective-permute-start = (bf16[2,5,2,128,128]{4,3,2,1,0:T(8,128)(2,1)}, bf16[2,5,2,128,128]{4,3,2,1,0:T(8,128)(2,1)}, u32[]{:S(2)}, u32[]{:S(2)}) collective-permute-start(bf16[2,5,2,128,128]{4,3,2,1,0:T(8,128)(2,1)} %bitcast.2), channel_id=1, source_target_pairs={{0,1},{1,0},{2,3},{3,2},{4,5},{5,4},{6,7},{7,6},{8,9},{9,8},{10,11... | collective-permute-start | bytes 1966088 | tf_op jit(solution)/shard_map/ppermute | solution.py:171
  5.2 5.0 %copy-start.1 = (bf16[1,2,5,2,128,128]{5,4,3,2,1,0:T(8,128)(2,1)S(1)}, bf16[1,2,5,2,128,128]{5,4,3,2,1,0:T(8,128)(2,1)}, u32[]{:S(2)}) copy-start(bf16[1,2,5,2,128,128]{5,4,3,2,1,0:T(8,128)(2,1)} %param.8) | copy-start | bytes 1966084
  5.2 22.3 %all-to-all-start = ((bf16[8,2,2,128,128]{4,3,2,1,0:T(8,128)(2,1)}), bf16[8,2,2,128,128]{4,3,2,1,0:T(8,128)(2,1)S(1)}, u32[]{:S(2)}, u32[]{:S(2)}) async-start(bf16[8,2,2,128,128]{4,3,2,1,0:T(8,128)(2,1)} %get-tuple-element.8), calls=%async_computation | async-start | bytes 2097152 | tf_op jit(solution)/shard_map/all_to_all | solution.py:385
  10.2 1.2 %copy-start = (s32[2,22]{1,0:T(2,128)S(1)}, s32[2,22]{1,0:T(2,128)}, u32[]{:S(2)}) copy-start(s32[2,22]{1,0:T(2,128)} %get-tuple-element.7.order_ref) | copy-start | bytes 532
  12.0 15.4 %collective-permute-start.1 = (bf16[2,2,128,128]{3,2,1,0:T(8,128)(2,1)S(1)}, bf16[2,2,128,128]{3,2,1,0:T(8,128)(2,1)S(1)}, u32[]{:S(2)}, u32[]{:S(2)}) collective-permute-start(bf16[2,2,128,128]{3,2,1,0:T(8,128)(2,1)S(1)} %shard_map.65), channel_id=1, source_target_pairs={{0,2},{1,3},{2,0},{3,1},{4,6},{5,7},{6,4},{7,5},{8,10},{9,11},{10,... | collective-permute-start | bytes 393224 | tf_op jit(solution)/shard_map/ppermute | solution.py:171
  29.1 8.8 %collective-permute-start.2 = (bf16[2,2,128,128]{3,2,1,0:T(8,128)(2,1)S(1)}, bf16[2,2,128,128]{3,2,1,0:T(8,128)(2,1)S(1)}, u32[]{:S(2)}, u32[]{:S(2)}) collective-permute-start(bf16[2,2,128,128]{3,2,1,0:T(8,128)(2,1)S(1)} %shard_map.67), channel_id=1, source_target_pairs={{0,16},{8,24},{16,0},{24,8},{1,17},{9,25},{17,1},{25,9},{2,18},{10... | collective-permute-start | bytes 393224 | tf_op jit(solution)/shard_map/ppermute | solution.py:392
  48.9 1.9 %collective-permute-start.3 = (bf16[4,2,2,128,128]{4,3,2,1,0:T(8,128)(2,1)S(1)}, bf16[4,2,2,128,128]{4,3,2,1,0:T(8,128)(2,1)S(1)}, u32[]{:S(2)}, u32[]{:S(2)}) collective-permute-start(bf16[4,2,2,128,128]{4,3,2,1,0:T(8,128)(2,1)S(1)} %all_to_all.10.same_ref), channel_id=1, source_target_pairs={{0,1},{1,0},{2,3},{3,2},{4,5},{5,4},{6,7},{7,6},{8,9},{9,8},{10,11... | collective-permute-start | bytes 1572872 | tf_op jit(solution)/shard_map/ppermute | solution.py:171

commit v6 on v3

--- a/solution.py
+++ b/solution.py
@@ -13,6 +13,7 @@
 SOURCES_AT_ONCE = 8
 COLUMNS = 192
 CORES = 2
+COPIES = 4
 IN_VMEM = pltpu.CompilerParams(vmem_limit_bytes=16 * 1024 * 1024)
 
 tanh_scale = math.sqrt(2.0 / math.pi)
@@ -100,31 +101,35 @@
 
 def pack_kernel(
     per_half, rows_ref, cols_ref, counts_ref, down_ref, up_ref,
-    out_ref, order_ref, flags_ref, first_ref, last_ref, sems,
+    out_ref, order_ref, flags_ref, whole, first_ref, last_ref, sems,
 ):
     slots, owners = cols_ref.shape[2], counts_ref.shape[2]
-    places, units = out_ref.shape[0], 2 * per_half
+    places, units, rows = out_ref.shape[0], 2 * per_half, whole.shape[1]
+    pieces = sems.shape[1]
     copies = []
-    used = [unit_place(unit, per_half, owners) for unit in range(units)]
-    for which, x_ref in ((1, up_ref), (0, down_ref)):
+    for which, x_ref in ((0, down_ref), (1, up_ref)):
+        for piece in range(pieces):
+            part = pl.ds(piece * (rows // pieces), rows // pieces)
+            copy = pltpu.make_async_copy(
+                x_ref.at[0, 0, part], whole.at[which, part], sems.at[which, piece]
+            )
+            copy.start()
+            copies.append(copy)
+    for which in range(2):
         order_units(
             cols_ref, counts_ref, which, slots, per_half, order_ref, flags_ref, first_ref, last_ref
         )
+    used = [unit_place(unit, per_half, owners) for unit in range(units)]
+    for place in range(places):
+        if place not in used:
+            out_ref[place] = jnp.zeros(out_ref.shape[1:], out_ref.dtype)
+    for which in range(2):
+        for copy in copies[which * pieces : (which + 1) * pieces]:
+            copy.wait()
         for i in range(2 * units):
             row = rows_ref[0, which, jnp.maximum(order_ref[which, i], 0)]
             at = pl.multiple_of(row * TILE, TILE)
-            copy = pltpu.make_async_copy(
-                x_ref.at[0, 0, :, pl.ds(at, TILE)],
-                out_ref.at[used[i // 2], which, i % 2],
-                sems.at[which, i],
-            )
-            copy.start()
-            copies.append(copy)
-    for place in range(places):
-        if place not in used:
-            out_ref[place] = jnp.zeros(out_ref.shape[1:], out_ref.dtype)
-    for copy in copies:
-        copy.wait()
+            out_ref[used[i // 2], which, i % 2] = whole[which, :, pl.ds(at, TILE)]
 
 
 def pack(x_down, x_up, tile_rows, tile_cols, counts, per_half, places):
@@ -142,12 +147,13 @@
         in_specs=[smem, smem, smem, hbm, hbm],
         out_specs=[vmem, smem, smem],
         scratch_shapes=[
+            pltpu.VMEM((2,) + x_down.shape[2:], x_down.dtype),
             pltpu.SMEM((COLUMNS + 1,), jnp.int32),
             pltpu.SMEM((COLUMNS + 1,), jnp.int32),
-            pltpu.SemaphoreType.DMA((2, 2 * units)),
+            pltpu.SemaphoreType.DMA((2, COPIES)),
         ],
         cost_estimate=pl.CostEstimate(
-            flops=0, bytes_accessed=16 * units * rows * TILE, transcendentals=0
+            flops=0, bytes_accessed=4 * x_down.size + 16 * units * rows * TILE, transcendentals=0
         ),
     )(tile_rows, tile_cols, counts, x_down, x_up)
 

time: 52 us -> 51.4 us (0.988)
  no operation moved by 1% of the time
where the time goes in v6:
time: 51.4 us; the launch traced here: 51.1 us
  waiting for transfers between devices  20 us (39%)
  blocking collectives  10.4 us (20%)
  starting transfers between devices  10.2 us (20%)
  Pallas kernels  9.23 us (18%)
  other arithmetic  1.21 us (2%)
    ppermute x3, waiting for transfers between devices, swapped(): return lax.ppermute(array, 'fsdp', [(i, i ^ apart) for i in range(size)])  15.2 us
    all_to_all x1, blocking collectives, body(): lax.all_to_all(mine, PLANE, split_axis=0, concat_axis=0, axis_index_group...  10.4 us
    all_to_all x1, starting transfers between devices, body(): lax.all_to_all(packed, PLANE, split_axis=0, concat_axis=0, tiled=True)  4.98 us
    ppermute x1, waiting for transfers between devices, body(): arrived = lax.ppermute(grads(1, dtype=jnp.bfloat16), 'section', across)  4.71 us
    pallas_call x1, Pallas kernels, pack(): pl.pallas_call(functools.partial(pack_kernel, per_half), out_shape=[jax.S...  3.74 us
    pallas_call x2, Pallas kernels, unit_grads(): pl.pallas_call(functools.partial(grads_kernel, which, per_half, owners, l...  3.38 us
    ppermute x1, starting transfers between devices, body(): arrived = lax.ppermute(grads(1, dtype=jnp.bfloat16), 'section', across)  2.65 us
    ppermute x3, starting transfers between devices, swapped(): return lax.ppermute(array, 'fsdp', [(i, i ^ apart) for i in range(size)])  2.53 us
  transfers between devices with their start and end apart: 5, of which 3 were waited for; matrix products, arithmetic and copies ran while one was open for 2% of the time, Pallas kernels for 12%

profile of v6, /device:TPU:0, one launch (start us, length us, event | category | flops | bytes accessed | tf_op | source)
XLA Modules:
  0.0 51.1 jit_solution(7237510022085097651)
XLA Ops:
  0.0 0.5 collective-permute-start
  0.5 3.7 %shard_map.64 = (bf16[8,2,2,128,128]{4,3,2,1,0:T(8,128)(2,1)}, s32[2,18]{1,0:T(2,128)}, s32[2,18]{1,0:T(2,128)}) custom-call(s32[1,2,20]{2,1,0:T(2,128)} %rows_ref.1, s32[1,2,20]{2,1,0:T(2,128)} %cols_ref.1, s32[1,2,4]{2,1,0:T(2,128)} %counts_ref.3, bf16[1,1,128,6144]{3,2,1,0:T(8,128)(2,1)} %down_ref.1, bf16[1,1,128,6144]{3,2,1,0:T(8,128)(2,1)} %up_ref.1), custom_call_target="tpu_custom_call" | custom-call | bytes 5242880 | tf_op jit(solution)/shard_map/pallas_call | solution.py:140
  4.2 0.0 copy-start.3
  4.2 5.0 %all-to-all-start = ((bf16[8,2,2,128,128]{4,3,2,1,0:T(8,128)(2,1)}), bf16[8,2,2,128,128]{4,3,2,1,0:T(8,128)(2,1)S(1)}, u32[]{:S(2)}, u32[]{:S(2)}) async-start(bf16[8,2,2,128,128]{4,3,2,1,0:T(8,128)(2,1)} %get-tuple-element.10), calls=%async_computation | async-start | bytes 2097152 | tf_op jit(solution)/shard_map/all_to_all | solution.py:377
  9.2 0.0 copy-start
  9.2 0.0 collective-permute-done
  9.2 0.0 copy-done.3
  9.2 1.2 %pad_maximum_fusion.near_ref = bf16[2,10,2,128,128]{4,3,2,1,0:T(8,128)(2,1)S(1)} fusion(bf16[2,5,2,128,128]{4,3,2,1,0:T(8,128)(2,1)} %collective-permute-done, bf16[2,5,2,128,128]{4,3,2,1,0:T(8,128)(2,1)S(1)} %bitcast.3), kind=kLoop, calls=%fused_computation | loop fusion | flops 655360 | bytes 2621440 | tf_op jit(solution)/shard_map/concatenate | solution.py:378
  10.4 0.0 copy-start.2
  10.4 0.0 copy-done
  10.4 0.6 %shard_map.65 = bf16[2,2,128,128]{3,2,1,0:T(8,128)(2,1)S(1)} custom-call(s32[2,18]{1,0:T(2,128)S(1)} %copy-done, bf16[2,10,2,128,128]{4,3,2,1,0:T(8,128)(2,1)S(1)} %pad_maximum_fusion.near_ref), custom_call_target="tpu_custom_call" | custom-call | bytes 300000 | tf_op jit(solution)/shard_map/pallas_call | solution.py:183
  11.1 2.1 %collective-permute-start.1 = (bf16[2,2,128,128]{3,2,1,0:T(8,128)(2,1)S(1)}, bf16[2,2,128,128]{3,2,1,0:T(8,128)(2,1)S(1)}, u32[]{:S(2)}, u32[]{:S(2)}) collective-permute-start(bf16[2,2,128,128]{3,2,1,0:T(8,128)(2,1)S(1)} %shard_map.65), channel_id=1, source_target_pairs={{0,2},{1,3},{2,0},{3,1},{4,6},{5,7},{6,4},{7,5},{8,10},{9,11},{10,... | collective-permute-start | bytes 393224 | tf_op jit(solution)/shard_map/ppermute | solution.py:163
  13.1 13.3 %collective-permute-done.1.far_ref = bf16[2,2,128,128]{3,2,1,0:T(8,128)(2,1)S(1)} collective-permute-done((bf16[2,2,128,128]{3,2,1,0:T(8,128)(2,1)S(1)}, bf16[2,2,128,128]{3,2,1,0:T(8,128)(2,1)S(1)}, u32[]{:S(2)}, u32[]{:S(2)}) %collective-permute-start.1) | collective-permute-done | bytes 131104 | tf_op jit(solution)/shard_map/ppermute | solution.py:163
  26.5 0.0 all-to-all-done.x_ref
  26.5 0.0 copy-done.2
  26.5 1.7 %shard_map.67 = bf16[2,2,128,128]{3,2,1,0:T(8,128)(2,1)S(1)} custom-call(s32[2,18]{1,0:T(2,128)S(1)} %copy-done, s32[2,18]{1,0:T(2,128)S(1)} %copy-done.2, bf16[8,2,2,128,128]{4,3,2,1,0:T(8,128)(2,1)S(1)} %all-to-all-done.x_ref, bf16[2,10,2,128,128]{4,3,2,1,0:T(8,128)(2,1)S(1)} %pad_maximum_fusion.near_ref, ...), custom_call_target="tpu_custom_call" | custom-call | flops 335544320 | bytes 524288 | tf_op jit(solution)/shard_map/pallas_call | solution.py:281
  28.2 2.7 %collective-permute-start.2 = (bf16[2,2,128,128]{3,2,1,0:T(8,128)(2,1)S(1)}, bf16[2,2,128,128]{3,2,1,0:T(8,128)(2,1)S(1)}, u32[]{:S(2)}, u32[]{:S(2)}) collective-permute-start(bf16[2,2,128,128]{3,2,1,0:T(8,128)(2,1)S(1)} %shard_map.67), channel_id=1, source_target_pairs={{0,16},{8,24},{16,0},{24,8},{1,17},{9,25},{17,1},{25,9},{2,18},{10... | collective-permute-start | bytes 393224 | tf_op jit(solution)/shard_map/ppermute | solution.py:384
  30.8 1.7 %shard_map.66.own_ref = f32[2,2,128,128]{3,2,1,0:T(8,128)S(1)} custom-call(s32[2,18]{1,0:T(2,128)S(1)} %copy-done, s32[2,18]{1,0:T(2,128)S(1)} %copy-done.2, bf16[8,2,2,128,128]{4,3,2,1,0:T(8,128)(2,1)S(1)} %all-to-all-done.x_ref, bf16[2,10,2,128,128]{4,3,2,1,0:T(8,128)(2,1)S(1)} %pad_maximum_fusion.near_ref, ...), custom_call_target="tpu_custom_call" | custom-call | flops 335544320 | bytes 524288 | tf_op jit(solution)/shard_map/pallas_call | solution.py:281
  32.5 0.0 copy-start.1
  32.5 4.7 %collective-permute-done.2.arrived_ref = bf16[2,2,128,128]{3,2,1,0:T(8,128)(2,1)S(1)} collective-permute-done((bf16[2,2,128,128]{3,2,1,0:T(8,128)(2,1)S(1)}, bf16[2,2,128,128]{3,2,1,0:T(8,128)(2,1)S(1)}, u32[]{:S(2)}, u32[]{:S(2)}) %collective-permute-start.2) | collective-permute-done | bytes 131104 | tf_op jit(solution)/shard_map/ppermute | solution.py:384
  37.3 10.4 %all_to_all.10.same_ref = bf16[4,2,2,128,128]{4,3,2,1,0:T(8,128)(2,1)S(1)} all-to-all(bf16[4,2,2,128,128]{4,3,2,1,0:T(8,128)(2,1)S(1)} %shard_map.68), channel_id=1, replica_groups={{0,2,4,6},{1,3,5,7},{8,10,12,14},{9,11,13,15},{16,18,20,22},{17,19,21,2..., dimensions={0} | all-to-all | bytes 1048576 | tf_op jit(solution)/shard_map/all_to_all | solution.py:389
  47.7 0.0 collective-permute-start.3
  47.7 1.9 %collective-permute-done.3.other_ref = bf16[4,2,2,128,128]{4,3,2,1,0:T(8,128)(2,1)S(1)} collective-permute-done((bf16[4,2,2,128,128]{4,3,2,1,0:T(8,128)(2,1)S(1)}, bf16[4,2,2,128,128]{4,3,2,1,0:T(8,128)(2,1)S(1)}, u32[]{:S(2)}, u32[]{:S(2)}) %collective-permute-start.3) | collective-permute-done | bytes 524320 | tf_op jit(solution)/shard_map/ppermute | solution.py:163
  49.6 0.0 copy-done.1
  49.6 1.5 %shard_map.69 = bf16[5,2,128,128]{3,2,1,0:T(8,128)(2,1)} custom-call(s32[2,18]{1,0:T(2,128)S(1)} %copy-done, s32[1,2,4]{2,1,0:T(2,128)S(1)} %copy-done.1, bf16[4,2,2,128,128]{4,3,2,1,0:T(8,128)(2,1)S(1)} %all_to_all.10.same_ref, bf16[4,2,2,128,128]{4,3,2,1,0:T(8,128)(2,1)S(1)} %collective-permute-done.3.other_ref), custom_call_target="tpu_custom_call" | custom-call | bytes 1000000 | tf_op jit(solution)/shard_map/pallas_call | solution.py:352
  (1 shorter events, 0.0 us)
Async XLA Ops:
  0.0 9.2 %collective-permute-start = (bf16[2,5,2,128,128]{4,3,2,1,0:T(8,128)(2,1)}, bf16[2,5,2,128,128]{4,3,2,1,0:T(8,128)(2,1)}, u32[]{:S(2)}, u32[]{:S(2)}) collective-permute-start(bf16[2,5,2,128,128]{4,3,2,1,0:T(8,128)(2,1)} %bitcast.2), channel_id=1, source_target_pairs={{0,1},{1,0},{2,3},{3,2},{4,5},{5,4},{6,7},{7,6},{8,9},{9,8},{10,11... | collective-permute-start | bytes 1966088 | tf_op jit(solution)/shard_map/ppermute | solution.py:163
  4.2 5.0 %copy-start.3 = (bf16[1,2,5,2,128,128]{5,4,3,2,1,0:T(8,128)(2,1)S(1)}, bf16[1,2,5,2,128,128]{5,4,3,2,1,0:T(8,128)(2,1)}, u32[]{:S(2)}) copy-start(bf16[1,2,5,2,128,128]{5,4,3,2,1,0:T(8,128)(2,1)} %param.8) | copy-start | bytes 1966084
  4.2 22.3 %all-to-all-start = ((bf16[8,2,2,128,128]{4,3,2,1,0:T(8,128)(2,1)}), bf16[8,2,2,128,128]{4,3,2,1,0:T(8,128)(2,1)S(1)}, u32[]{:S(2)}, u32[]{:S(2)}) async-start(bf16[8,2,2,128,128]{4,3,2,1,0:T(8,128)(2,1)} %get-tuple-element.10), calls=%async_computation | async-start | bytes 2097152 | tf_op jit(solution)/shard_map/all_to_all | solution.py:377
  9.2 1.2 %copy-start = (s32[2,18]{1,0:T(2,128)S(1)}, s32[2,18]{1,0:T(2,128)}, u32[]{:S(2)}) copy-start(s32[2,18]{1,0:T(2,128)} %get-tuple-element.8.order_ref) | copy-start | bytes 436
  10.4 16.0 %copy-start.2 = (s32[2,18]{1,0:T(2,128)S(1)}, s32[2,18]{1,0:T(2,128)}, u32[]{:S(2)}) copy-start(s32[2,18]{1,0:T(2,128)} %get-tuple-element.9.flags_ref) | copy-start | bytes 436
  11.1 15.4 %collective-permute-start.1 = (bf16[2,2,128,128]{3,2,1,0:T(8,128)(2,1)S(1)}, bf16[2,2,128,128]{3,2,1,0:T(8,128)(2,1)S(1)}, u32[]{:S(2)}, u32[]{:S(2)}) collective-permute-start(bf16[2,2,128,128]{3,2,1,0:T(8,128)(2,1)S(1)} %shard_map.65), channel_id=1, source_target_pairs={{0,2},{1,3},{2,0},{3,1},{4,6},{5,7},{6,4},{7,5},{8,10},{9,11},{10,... | collective-permute-start | bytes 393224 | tf_op jit(solution)/shard_map/ppermute | solution.py:163
  28.2 9.1 %collective-permute-start.2 = (bf16[2,2,128,128]{3,2,1,0:T(8,128)(2,1)S(1)}, bf16[2,2,128,128]{3,2,1,0:T(8,128)(2,1)S(1)}, u32[]{:S(2)}, u32[]{:S(2)}) collective-permute-start(bf16[2,2,128,128]{3,2,1,0:T(8,128)(2,1)S(1)} %shard_map.67), channel_id=1, source_target_pairs={{0,16},{8,24},{16,0},{24,8},{1,17},{9,25},{17,1},{25,9},{2,18},{10... | collective-permute-start | bytes 393224 | tf_op jit(solution)/shard_map/ppermute | solution.py:384
  32.5 17.1 %copy-start.1 = (s32[1,2,4]{2,1,0:T(2,128)S(1)}, s32[1,2,4]{2,1,0:T(2,128)}, u32[]{:S(2)}) copy-start(s32[1,2,4]{2,1,0:T(2,128)} %counts_ref.3) | copy-start | bytes 100
  47.7 1.9 %collective-permute-start.3 = (bf16[4,2,2,128,128]{4,3,2,1,0:T(8,128)(2,1)S(1)}, bf16[4,2,2,128,128]{4,3,2,1,0:T(8,128)(2,1)S(1)}, u32[]{:S(2)}, u32[]{:S(2)}) collective-permute-start(bf16[4,2,2,128,128]{4,3,2,1,0:T(8,128)(2,1)S(1)} %all_to_all.10.same_ref), channel_id=1, source_target_pairs={{0,1},{1,0},{2,3},{3,2},{4,5},{5,4},{6,7},{7,6},{8,9},{9,8},{10,11... | collective-permute-start | bytes 1572872 | tf_op jit(solution)/shard_map/ppermute | solution.py:163
